TPU v7x, 512 devices: a whole 4x8x8 slice. The times are simulated.
512 devices in a mesh: view: 4 (over x), dev: 128 (over y, z, core).
Axes of the slice: x: 4, y: 8, z: 8, core: 2. Of those that a mesh axis runs over, the one named last changes fastest.
Arguments:
- params: float32 [59, 524288], P(None, 'dev'), may hold values from -6 to 2.8, as said below
- first_moment: float32 [59, 524288], P(None, 'dev'), may hold values from -0.3 to 0.3
- second_moment: float32 [59, 524288], P(None, 'dev'), may hold values from 0.0001 to 0.01
- cam_centers: float32 [4, 3], P('view'), may hold values from -4 to 0.7, as said below
- target: float32 [4, 2048, 3, 256], P('view', 'dev'), may hold values from 0 to 1
- send_rows: int32 [4, 128, 1024], P('view', 'dev'), may hold values from 0 to 4095, as said below
- tile_lists: int32 [4, 2048, 64], P('view', 'dev'), may hold values from 0 to 1023, as said below
- tile_counts: int32 [4, 2048], P('view', 'dev'), may hold values from 1 to 64, as said below
- tile_ids: int32 [4, 2048], P('view', 'dev'), may hold values from 0 to 2047, as said below
- move_order: int32 [128, 4096], P('dev'), may hold values from 0 to 4095, each once within a row
Outputs:
- new_params: float32 [59, 524288], P(None, 'dev')
- new_first: float32 [59, 524288], P(None, 'dev')
- new_second: float32 [59, 524288], P(None, 'dev')
Inputs may be any that keep to these rules, and one draw needn't show every extreme that they name: `cam_centers`: for every view the first two coordinates lie in 0.3 to 0.7 and the third in -4 to -2. `params`: rows 0 and 1 lie in -1.8 to 2.8, row 2 in 0 to 1, rows 3 to 5 in -5 to -3, row 6 in 0.5 to 1.5, rows 7 to 9 in -1 to 1, row 10 in -6 to -3, rows 11 to 58 in -1.5 to 1.5. `send_rows`: each of an owner's 4096 Gaussians fills exactly one of its slots over all views and renderers. `tile_lists`: the list of tile slot k names each of its renderer's slots (k % 16) * 64 to (k % 16 + 1) * 64 - 1 exactly once. `tile_counts`: some tile of every view has a full list. Each view's tile_ids is a permutation.
All inputs are finite; a program needn't handle non-finite values.
Results may differ from a plain program's by a relative error of at most 0.0003.
Values sent between devices are 32-bit elements; how exact they have to be, the bound alone decides.
A program may use at most 64 MiB of HBM per device.

v0:
```python
import jax
import jax.numpy as jnp
from jax import lax
from jax.sharding import PartitionSpec as P

PARAMS = 59
FEATS = 9
TILE_SIDE = 16
TILES_X = 64
BLOCK = 32
MOVE_PEER = 1
ADAM_STEP = 1000


FOCAL_LEN = 1.2
DILATION = 0.3
SH_C0 = 0.28209479177387814
SH_C1 = 0.4886025119029199
SH_C2 = (
    1.0925484305920792,
    -1.0925484305920792,
    0.31539156525252005,
    -1.0925484305920792,
    0.5462742152960396,
)
SH_C3 = (
    -0.5900435899266435,
    2.890611442640554,
    -0.4570457994644658,
    0.3731763325901154,
    -0.4570457994644658,
    1.445305721320277,
    -0.5900435899266435,
)
BETA_ONE = 0.9
BETA_TWO = 0.999
ADAM_EPS = 1e-08


def sh_basis(dir_x, dir_y, dir_z):
    dir_xx = dir_x * dir_x
    dir_yy = dir_y * dir_y
    dir_zz = dir_z * dir_z
    return jnp.stack(
        [
            SH_C0 + 0.0 * dir_x,
            -SH_C1 * dir_y,
            SH_C1 * dir_z,
            -SH_C1 * dir_x,
            SH_C2[0] * dir_x * dir_y,
            SH_C2[1] * dir_y * dir_z,
            SH_C2[2] * (2.0 * dir_zz - dir_xx - dir_yy),
            SH_C2[3] * dir_x * dir_z,
            SH_C2[4] * (dir_xx - dir_yy),
            SH_C3[0] * dir_y * (3.0 * dir_xx - dir_yy),
            SH_C3[1] * dir_x * dir_y * dir_z,
            SH_C3[2] * dir_y * (4.0 * dir_zz - dir_xx - dir_yy),
            SH_C3[3] * dir_z * (2.0 * dir_zz - 3.0 * dir_xx - 3.0 * dir_yy),
            SH_C3[4] * dir_x * (4.0 * dir_zz - dir_xx - dir_yy),
            SH_C3[5] * dir_z * (dir_xx - dir_yy),
            SH_C3[6] * dir_x * (dir_xx - 3.0 * dir_yy),
        ]
    )


def project(values, center, width_px, height_px):
    offset = values[0:3] - center[:, None]
    inverse = 1.0 / offset[2]
    mean_u = 0.5 + FOCAL_LEN * offset[0] * inverse
    mean_v = 0.5 + FOCAL_LEN * offset[1] * inverse
    scale_sq = jnp.exp(2.0 * values[3:6])
    quaternion = values[6:10]
    quaternion = quaternion * lax.rsqrt(jnp.sum(quaternion * quaternion, axis=0, keepdims=True))
    quat_w, quat_x, quat_y, quat_z = (quaternion[0], quaternion[1], quaternion[2], quaternion[3])
    rotation = [
        [
            1.0 - 2.0 * (quat_y * quat_y + quat_z * quat_z),
            2.0 * (quat_x * quat_y - quat_w * quat_z),
            2.0 * (quat_x * quat_z + quat_w * quat_y),
        ],
        [
            2.0 * (quat_x * quat_y + quat_w * quat_z),
            1.0 - 2.0 * (quat_x * quat_x + quat_z * quat_z),
            2.0 * (quat_y * quat_z - quat_w * quat_x),
        ],
        [
            2.0 * (quat_x * quat_z - quat_w * quat_y),
            2.0 * (quat_y * quat_z + quat_w * quat_x),
            1.0 - 2.0 * (quat_x * quat_x + quat_y * quat_y),
        ],
    ]
    focal_now = FOCAL_LEN * inverse
    slope_u = -focal_now * offset[0] * inverse
    slope_v = -focal_now * offset[1] * inverse
    cov_uu = DILATION / (width_px * width_px)
    cov_vv = DILATION / (height_px * height_px)
    cov_uv = 0.0
    for column in range(3):
        axis_u = focal_now * rotation[0][column] + slope_u * rotation[2][column]
        axis_v = focal_now * rotation[1][column] + slope_v * rotation[2][column]
        cov_uu = cov_uu + axis_u * axis_u * scale_sq[column]
        cov_vv = cov_vv + axis_v * axis_v * scale_sq[column]
        cov_uv = cov_uv + axis_u * axis_v * scale_sq[column]
    determinant = cov_uu * cov_vv - cov_uv * cov_uv
    distance = jnp.sqrt(jnp.sum(offset * offset, axis=0))
    sh_values = sh_basis(offset[0] / distance, offset[1] / distance, offset[2] / distance)
    sh_coef = values[11:].reshape(16, 3, values.shape[1])
    colors = 0.5 + jnp.sum(sh_values[:, None, :] * sh_coef, axis=0)
    opacity = jax.nn.sigmoid(values[10])
    return jnp.concatenate(
        [
            jnp.stack(
                [mean_u, mean_v, cov_vv / determinant, -cov_uv / determinant, cov_uu / determinant]
            ),
            colors,
            opacity[None, :],
        ],
        axis=0,
    )


def pixel_coords(tile_id, width_px, height_px):
    within = jnp.arange(TILE_SIDE * TILE_SIDE, dtype=jnp.int32)
    pixel_col = tile_id % TILES_X * TILE_SIDE + within % TILE_SIDE
    pixel_row = tile_id // TILES_X * TILE_SIDE + within // TILE_SIDE
    return (
        (pixel_col.astype(jnp.float32) + 0.5) / width_px,
        (pixel_row.astype(jnp.float32) + 0.5) / height_px,
    )


def learning_rates():
    rows_all = jnp.arange(PARAMS, dtype=jnp.int32)
    return jnp.where(
        rows_all < 3,
        0.00016,
        jnp.where(
            rows_all < 6,
            0.005,
            jnp.where(
                rows_all < 10,
                0.001,
                jnp.where(rows_all < 11, 0.05, jnp.where(rows_all < 14, 0.0025, 0.000125)),
            ),
        ),
    )


def adam_update(values, moment_one, moment_two, gradient, step_sizes):
    bias_one = 1.0 - BETA_ONE**ADAM_STEP
    bias_two = 1.0 - BETA_TWO**ADAM_STEP
    new_one = BETA_ONE * moment_one + (1.0 - BETA_ONE) * gradient
    new_two = BETA_TWO * moment_two + (1.0 - BETA_TWO) * gradient * gradient
    updated = values - step_sizes * (new_one / bias_one) / (jnp.sqrt(new_two / bias_two) + ADAM_EPS)
    return (updated, new_one, new_two)


def render_blocks(features, list_count, tile_id, width_px, height_px, triangle):
    pixel_u, pixel_v = pixel_coords(tile_id, width_px, height_px)
    block_total = features.shape[1] // BLOCK
    in_blocks = features.reshape(FEATS, block_total, BLOCK).transpose(1, 0, 2)
    block_starts = jnp.arange(block_total, dtype=jnp.int32) * BLOCK

    def advance(carried, one_block, block_start):
        log_trans, rendered = carried
        is_live = block_start + jnp.arange(BLOCK, dtype=jnp.int32) < list_count
        diff_u = pixel_u[:, None] - one_block[0][None, :]
        diff_v = pixel_v[:, None] - one_block[1][None, :]
        exponent = (
            -0.5 * (one_block[2] * diff_u * diff_u + one_block[4] * diff_v * diff_v)
            - one_block[3] * diff_u * diff_v
        )
        alphas = jnp.where(is_live[None, :], one_block[8][None, :] * jnp.exp(exponent), 0.0)
        log_keep = jnp.log1p(-alphas)
        before = jnp.dot(log_keep, triangle, precision=lax.Precision.HIGHEST) + log_trans[:, None]
        weight = alphas * jnp.exp(before)
        added = lax.dot_general(
            one_block[5:8], weight, (((1,), (1,)), ((), ())), precision=lax.Precision.HIGHEST
        )
        return (log_trans + jnp.sum(log_keep, axis=1), rendered + added)

    advance = jax.checkpoint(advance)

    def block_step(carried, block_item):
        one_block, block_start = block_item
        advanced = advance(carried, one_block, block_start)
        return (advanced, None)

    start_pair = (
        jnp.zeros((TILE_SIDE * TILE_SIDE,), jnp.float32),
        jnp.zeros((3, TILE_SIDE * TILE_SIDE), jnp.float32),
    )
    final_pair = lax.scan(block_step, start_pair, (in_blocks, block_starts))[0]
    return final_pair[1]


def per_device(
    params,
    first_moment,
    second_moment,
    cam_centers,
    target,
    send_rows,
    tile_lists,
    tile_counts,
    tile_ids,
    move_order,
):
    owners = lax.axis_size("dev")
    tiles_here = tile_lists.shape[1]
    width_px = float(TILES_X * TILE_SIDE)
    height_px = float(owners * tiles_here // TILES_X * TILE_SIDE)
    rows_here = send_rows[0, 0]
    center = cam_centers[0]
    outgoing, pull_back = jax.vjp(
        lambda values: project(values, center, width_px, height_px)[:, rows_here], params
    )
    arrived = lax.all_to_all(outgoing, "dev", split_axis=1, concat_axis=1, tiled=True)
    triangle = (
        lax.broadcasted_iota(jnp.int32, (BLOCK, BLOCK), 0)
        < lax.broadcasted_iota(jnp.int32, (BLOCK, BLOCK), 1)
    ).astype(jnp.float32)

    def one_tile(tile_index, slot_grads):
        entries = tile_lists[0, tile_index]
        list_count = tile_counts[0, tile_index]
        tile_id = tile_ids[0, tile_index]
        gathered = arrived[:, entries]
        rendered, tile_back = jax.vjp(
            lambda features: render_blocks(
                features, list_count, tile_id, width_px, height_px, triangle
            ),
            gathered,
        )
        feat_grads = tile_back(rendered - target[0, tile_index])[0]
        return slot_grads.at[:, entries].add(feat_grads)

    slot_grads = lax.fori_loop(
        0, tiles_here, one_tile, jnp.zeros((FEATS, arrived.shape[1]), jnp.float32)
    )
    returned = lax.all_to_all(slot_grads, "dev", split_axis=1, concat_axis=1, tiled=True)
    view_grads = pull_back(returned)[0]
    step_sizes = learning_rates()[:, None]
    gradient = lax.psum(view_grads, "view")
    updated, new_one, new_two = adam_update(
        params, first_moment, second_moment, gradient, step_sizes
    )
    new_order = move_order[0]
    keep_rows = new_order.shape[0] - owners * MOVE_PEER
    ordered_params = updated[:, new_order]
    ordered_one = new_one[:, new_order]
    ordered_two = new_two[:, new_order]
    moved = (
        lax.all_to_all(
            ordered_params[:, keep_rows:], "dev", split_axis=1, concat_axis=1, tiled=True
        ),
        lax.all_to_all(ordered_one[:, keep_rows:], "dev", split_axis=1, concat_axis=1, tiled=True),
        lax.all_to_all(ordered_two[:, keep_rows:], "dev", split_axis=1, concat_axis=1, tiled=True),
    )
    return (
        jnp.concatenate([ordered_params[:, :keep_rows], moved[0]], axis=1),
        jnp.concatenate([ordered_one[:, :keep_rows], moved[1]], axis=1),
        jnp.concatenate([ordered_two[:, :keep_rows], moved[2]], axis=1),
    )


def solution(mesh):
    placed = (
        P(None, "dev"),
        P(None, "dev"),
        P(None, "dev"),
        P("view", None),
        P("view", "dev", None, None),
        P("view", "dev", None),
        P("view", "dev", None),
        P("view", "dev"),
        P("view", "dev"),
        P("dev", None),
    )
    return jax.shard_map(
        per_device,
        mesh=mesh,
        in_specs=placed,
        out_specs=(P(None, "dev"), P(None, "dev"), P(None, "dev")),
        check_vma=False,
    )
```

profile of v0, /device:TPU:1, one launch (start us, length us, event | category | flops | bytes accessed | tf_op | source)
XLA Modules:
  0.0 652.6 jit_solution(17421301210983496005)
XLA Ops:
  25.6 18.4 %all-to-all-start = ((f32[9,128,8]{0,2,1:T(8,128)}), f32[9,128,8]{0,2,1:T(8,128)S(1)}, u32[]{:S(2)}, u32[]{:S(2)}) async-start(f32[9,128,8]{0,2,1:T(8,128)} %bitcast.205), calls=%async_computation | async-start | bytes 1048576 | tf_op jit(solution)/shard_map/all_to_all | solution.py:218
  44.0 19.5 %all-to-all-done = f32[9,128,8]{0,2,1:T(8,128)S(1)} async-done(((f32[9,128,8]{0,2,1:T(8,128)}), f32[9,128,8]{0,2,1:T(8,128)S(1)}, u32[]{:S(2)}, u32[]{:S(2)}) %all-to-all-start) | async-done | bytes 36896 | tf_op jit(solution)/shard_map/all_to_all | solution.py:218
  64.3 329.7 %while.125 = (s32[]{:T(128)}, f32[9,1024]{0,1:T(8,128)}, s32[1,16,64]{2,1,0:T(8,128)}, f32[9,1024]{0,1:T(8,128)S(1)}, s32[1,16]{1,0:T(1,128)}, /*index=5*/s32[1,...) while((s32[]{:T(128)}, f32[9,1024]{0,1:T(8,128)}, ...), condition=%wide.region_17.18_spmd.clone.clone, body=%wide.region_3.17_spmd.clone.clone.sunk | while | flops 11585766 | bytes 575083 | solution.py:238
  75.3 6.7 %while.127 = (s32[]{:T(128)}, f32[256]{0:T(256)S(1)}, f32[3,256]{1,0:T(4,128)S(1)}, f32[2,9,32]{2,1,0:T(8,128)S(1)}, f32[2,256]{1,0:T(2,128)S(1)}, /*index=5*/f3...) while((s32[]{:T(128)}, f32[256]{0:T(256)S(1)}, ...), condition=%wide.region_15.15_spmd.clone.clone, body=%wide.region_7.14_spmd.clone.clone.sunk | while | flops 7773060 | bytes 420579 | solution.py:193
  96.0 6.7 %while.127 = (s32[]{:T(128)}, f32[256]{0:T(256)S(1)}, f32[3,256]{1,0:T(4,128)S(1)}, f32[2,9,32]{2,1,0:T(8,128)S(1)}, f32[2,256]{1,0:T(2,128)S(1)}, /*index=5*/f3...) while((s32[]{:T(128)}, f32[256]{0:T(256)S(1)}, ...), condition=%wide.region_15.15_spmd.clone.clone, body=%wide.region_7.14_spmd.clone.clone.sunk | while | flops 7773060 | bytes 420579 | solution.py:193
  116.6 6.7 %while.127 = (s32[]{:T(128)}, f32[256]{0:T(256)S(1)}, f32[3,256]{1,0:T(4,128)S(1)}, f32[2,9,32]{2,1,0:T(8,128)S(1)}, f32[2,256]{1,0:T(2,128)S(1)}, /*index=5*/f3...) while((s32[]{:T(128)}, f32[256]{0:T(256)S(1)}, ...), condition=%wide.region_15.15_spmd.clone.clone, body=%wide.region_7.14_spmd.clone.clone.sunk | while | flops 7773060 | bytes 420579 | solution.py:193
  137.2 6.7 %while.127 = (s32[]{:T(128)}, f32[256]{0:T(256)S(1)}, f32[3,256]{1,0:T(4,128)S(1)}, f32[2,9,32]{2,1,0:T(8,128)S(1)}, f32[2,256]{1,0:T(2,128)S(1)}, /*index=5*/f3...) while((s32[]{:T(128)}, f32[256]{0:T(256)S(1)}, ...), condition=%wide.region_15.15_spmd.clone.clone, body=%wide.region_7.14_spmd.clone.clone.sunk | while | flops 7773060 | bytes 420579 | solution.py:193
  157.8 6.7 %while.127 = (s32[]{:T(128)}, f32[256]{0:T(256)S(1)}, f32[3,256]{1,0:T(4,128)S(1)}, f32[2,9,32]{2,1,0:T(8,128)S(1)}, f32[2,256]{1,0:T(2,128)S(1)}, /*index=5*/f3...) while((s32[]{:T(128)}, f32[256]{0:T(256)S(1)}, ...), condition=%wide.region_15.15_spmd.clone.clone, body=%wide.region_7.14_spmd.clone.clone.sunk | while | flops 7773060 | bytes 420579 | solution.py:193
  178.4 6.7 %while.127 = (s32[]{:T(128)}, f32[256]{0:T(256)S(1)}, f32[3,256]{1,0:T(4,128)S(1)}, f32[2,9,32]{2,1,0:T(8,128)S(1)}, f32[2,256]{1,0:T(2,128)S(1)}, /*index=5*/f3...) while((s32[]{:T(128)}, f32[256]{0:T(256)S(1)}, ...), condition=%wide.region_15.15_spmd.clone.clone, body=%wide.region_7.14_spmd.clone.clone.sunk | while | flops 7773060 | bytes 420579 | solution.py:193
  219.6 6.7 %while.127 = (s32[]{:T(128)}, f32[256]{0:T(256)S(1)}, f32[3,256]{1,0:T(4,128)S(1)}, f32[2,9,32]{2,1,0:T(8,128)S(1)}, f32[2,256]{1,0:T(2,128)S(1)}, /*index=5*/f3...) while((s32[]{:T(128)}, f32[256]{0:T(256)S(1)}, ...), condition=%wide.region_15.15_spmd.clone.clone, body=%wide.region_7.14_spmd.clone.clone.sunk | while | flops 7773060 | bytes 420579 | solution.py:193
  260.8 6.7 %while.127 = (s32[]{:T(128)}, f32[256]{0:T(256)S(1)}, f32[3,256]{1,0:T(4,128)S(1)}, f32[2,9,32]{2,1,0:T(8,128)S(1)}, f32[2,256]{1,0:T(2,128)S(1)}, /*index=5*/f3...) while((s32[]{:T(128)}, f32[256]{0:T(256)S(1)}, ...), condition=%wide.region_15.15_spmd.clone.clone, body=%wide.region_7.14_spmd.clone.clone.sunk | while | flops 7773060 | bytes 420579 | solution.py:193
  281.4 6.7 %while.127 = (s32[]{:T(128)}, f32[256]{0:T(256)S(1)}, f32[3,256]{1,0:T(4,128)S(1)}, f32[2,9,32]{2,1,0:T(8,128)S(1)}, f32[2,256]{1,0:T(2,128)S(1)}, /*index=5*/f3...) while((s32[]{:T(128)}, f32[256]{0:T(256)S(1)}, ...), condition=%wide.region_15.15_spmd.clone.clone, body=%wide.region_7.14_spmd.clone.clone.sunk | while | flops 7773060 | bytes 420579 | solution.py:193
  302.0 6.7 %while.127 = (s32[]{:T(128)}, f32[256]{0:T(256)S(1)}, f32[3,256]{1,0:T(4,128)S(1)}, f32[2,9,32]{2,1,0:T(8,128)S(1)}, f32[2,256]{1,0:T(2,128)S(1)}, /*index=5*/f3...) while((s32[]{:T(128)}, f32[256]{0:T(256)S(1)}, ...), condition=%wide.region_15.15_spmd.clone.clone, body=%wide.region_7.14_spmd.clone.clone.sunk | while | flops 7773060 | bytes 420579 | solution.py:193
  343.2 6.7 %while.127 = (s32[]{:T(128)}, f32[256]{0:T(256)S(1)}, f32[3,256]{1,0:T(4,128)S(1)}, f32[2,9,32]{2,1,0:T(8,128)S(1)}, f32[2,256]{1,0:T(2,128)S(1)}, /*index=5*/f3...) while((s32[]{:T(128)}, f32[256]{0:T(256)S(1)}, ...), condition=%wide.region_15.15_spmd.clone.clone, body=%wide.region_7.14_spmd.clone.clone.sunk | while | flops 7773060 | bytes 420579 | solution.py:193
  394.0 8.3 %all-to-all-start.1 = ((f32[9,128,8]{0,2,1:T(8,128)}), f32[9,128,8]{0,2,1:T(8,128)}, u32[]{:S(2)}, u32[]{:S(2)}) async-start(f32[9,128,8]{0,2,1:T(8,128)} %bitcast.8), calls=%async_computation.1 | async-start | bytes 1048576 | tf_op jit(solution)/shard_map/all_to_all | solution.py:241
  402.9 18.6 %all-to-all-done.1 = f32[9,128,8]{0,2,1:T(8,128)} async-done(((f32[9,128,8]{0,2,1:T(8,128)}), f32[9,128,8]{0,2,1:T(8,128)}, u32[]{:S(2)}, u32[]{:S(2)}) %all-to-all-start.1) | async-done | bytes 36896 | tf_op jit(solution)/shard_map/all_to_all | solution.py:241
  438.8 7.3 %fusion.148 = (f32[1,4096]{0,1:T(8,128)}, f32[1,4096]{0,1:T(8,128)}, f32[1,4096]{0,1:T(8,128)}, f32[1,4096]{0,1:T(8,128)}, f32[1,4096]{0,1:T(8,128)}, /*index=5*/f32[1,4096]{0,1:T(8,128)}) fusion(f32[9,4096]{0,1:T(8,128)S(1)} %scatter_custom_fusion.1), kind=kLoop, calls=%fused_computation.359 | loop fusion | bytes 196608 | tf_op jit(solution)/shard_map/transpose(jvp())/split | solution.py:110
  472.7 48.9 %all-reduce.35.cloned.1.call-done = f32[59,4096]{1,0:T(8,128)} async-done(((f32[59,4096]{1,0:T(8,128)}), f32[59,4096]{1,0:T(8,128)}) %all-reduce.35.cloned.1.call-update) | async-done | bytes 966672 | tf_op jit(solution)/shard_map/psum | solution.py:244
  526.7 14.1 %gather_fusion.2 = f32[4096,59]{1,0:T(8,128)} fusion(f32[59,4096]{0,1:T(8,128)S(1)} %copy.218, s32[4096]{0:T(1024)S(1)} %broadcast_clamp_fusion), kind=kCustom, calls=%fused_computation.2 | custom fusion | bytes 1949696 | tf_op jit(solution)/shard_map/gather | solution.py:250
  542.3 16.0 %all-to-all-start.2 = ((f32[59,128,1]{0,2,1:T(1,128)}), f32[59,128,1]{0,2,1:T(1,128)S(1)}, u32[]{:S(2)}, u32[]{:S(2)}) async-start(f32[59,128,1]{0,2,1:T(1,128)} %bitcast.35), calls=%async_computation.2 | async-start | bytes 131072 | tf_op jit(solution)/shard_map/all_to_all | solution.py:254
  562.0 14.1 %gather_fusion.3 = f32[4096,59]{1,0:T(8,128)} fusion(f32[59,4096]{0,1:T(8,128)S(1)} %copy.220, s32[4096]{0:T(1024)S(1)} %broadcast_clamp_fusion), kind=kCustom, calls=%fused_computation.3 | custom fusion | bytes 1949696 | tf_op jit(solution)/shard_map/gather | solution.py:251
  581.3 14.1 %gather_fusion.4 = f32[4096,59]{1,0:T(8,128)} fusion(f32[59,4096]{0,1:T(8,128)S(1)} %copy.222, s32[4096]{0:T(1024)S(1)} %broadcast_clamp_fusion), kind=kCustom, calls=%fused_computation.4 | custom fusion | bytes 1949696 | tf_op jit(solution)/shard_map/gather | solution.py:252
  599.9 13.7 %all-to-all-start.3 = ((f32[59,128,1]{0,2,1:T(1,128)}), f32[59,128,1]{0,2,1:T(1,128)S(1)}, u32[]{:S(2)}, u32[]{:S(2)}) async-start(f32[59,128,1]{0,2,1:T(1,128)} %bitcast.39), calls=%async_computation.3 | async-start | bytes 131072 | tf_op jit(solution)/shard_map/all_to_all | solution.py:257
  615.4 9.7 %all-to-all-done.3 = f32[59,128,1]{0,2,1:T(1,128)S(1)} async-done(((f32[59,128,1]{0,2,1:T(1,128)}), f32[59,128,1]{0,2,1:T(1,128)S(1)}, u32[]{:S(2)}, u32[]{:S(2)}) %all-to-all-start.3) | async-done | bytes 30240 | tf_op jit(solution)/shard_map/all_to_all | solution.py:257
  (1269 shorter events, 503.7 us)
Async XLA Ops:
  18.1 7.5 %copy-start.33 = (f32[1,4096]{1,0:T(1,128)}, f32[1,4096]{1,0:T(1,128)S(1)}, u32[]{:S(2)}) copy-start(f32[1,4096]{1,0:T(1,128)S(1)} %get-tuple-element.1109) | copy-start | bytes 49156
  25.6 37.9 %all-to-all-start = ((f32[9,128,8]{0,2,1:T(8,128)}), f32[9,128,8]{0,2,1:T(8,128)S(1)}, u32[]{:S(2)}, u32[]{:S(2)}) async-start(f32[9,128,8]{0,2,1:T(8,128)} %bitcast.205), calls=%async_computation | async-start | bytes 1048576 | tf_op jit(solution)/shard_map/all_to_all | solution.py:218
  394.0 27.5 %all-to-all-start.1 = ((f32[9,128,8]{0,2,1:T(8,128)}), f32[9,128,8]{0,2,1:T(8,128)}, u32[]{:S(2)}, u32[]{:S(2)}) async-start(f32[9,128,8]{0,2,1:T(8,128)} %bitcast.8), calls=%async_computation.1 | async-start | bytes 1048576 | tf_op jit(solution)/shard_map/all_to_all | solution.py:241
  402.3 119.3 %all-reduce.35.cloned.1.call-start = ((), (), s32[]{:S(2)}) async-start(), calls=%async_computation.5 | async-start | bytes 2097152 | tf_op jit(solution)/shard_map/psum | solution.py:244
  438.8 7.3 %copy-start.3 = (f32[16,3,4096]{2,1,0:T(4,128)S(1)}, f32[16,3,4096]{2,1,0:T(4,128)}, u32[]{:S(2)}) copy-start(f32[16,3,4096]{2,1,0:T(4,128)} %get-tuple-element.1045) | copy-start | bytes 2359300
  454.4 5.8 copy-start.27
  454.4 5.8 copy-start.28
  454.5 9.9 %copy-start = (f32[1,4096]{0,1:T(8,128)S(1)}, f32[1,4096]{0,1:T(8,128)}, u32[]{:S(2)}) copy-start(f32[1,4096]{0,1:T(8,128)} %get-tuple-element.1012) | copy-start | bytes 49156
  460.2 6.1 copy-start.2
  460.2 7.0 %copy-start.22 = (f32[4096]{0:T(1024)S(1)}, f32[4096]{0:T(1024)}, u32[]{:S(2)}) copy-start(f32[4096]{0:T(1024)} %copy-done.21) | copy-start | bytes 49156
  462.3 8.0 %copy-start.24 = (f32[4096]{0:T(1024)S(1)}, f32[4096]{0:T(1024)}, u32[]{:S(2)}) copy-start(f32[4096]{0:T(1024)} %copy-done.23) | copy-start | bytes 49156
  463.7 6.6 %copy-start.36 = (f32[1,4096]{1,0:T(1,128)S(1)}, f32[1,4096]{1,0:T(1,128)}, u32[]{:S(2)}) copy-start(f32[1,4096]{1,0:T(1,128)} %get-tuple-element.1050) | copy-start | bytes 49156
  464.3 7.0 %copy-start.37 = (f32[1,4096]{1,0:T(1,128)S(1)}, f32[1,4096]{1,0:T(1,128)}, u32[]{:S(2)}) copy-start(f32[1,4096]{1,0:T(1,128)} %get-tuple-element.1015) | copy-start | bytes 49156
  464.4 7.1 %copy-start.35 = (f32[1,4096]{1,0:T(1,128)S(1)}, f32[1,4096]{1,0:T(1,128)}, u32[]{:S(2)}) copy-start(f32[1,4096]{1,0:T(1,128)} %fusion.105) | copy-start | bytes 49156
  465.0 6.4 copy-start.38
  465.0 6.4 copy-start.39
  465.0 6.5 copy-start.6
  469.2 52.4 %copy-start.7 = (f32[59,4096]{1,0:T(8,128)S(1)}, f32[59,4096]{1,0:T(8,128)}, u32[]{:S(2)}) copy-start(f32[59,4096]{1,0:T(8,128)} %param.17) | copy-start | bytes 2899972
  469.2 52.4 %copy-start.8 = (f32[59,4096]{1,0:T(8,128)S(1)}, f32[59,4096]{1,0:T(8,128)}, u32[]{:S(2)}) copy-start(f32[59,4096]{1,0:T(8,128)} %param.18) | copy-start | bytes 2899972
  469.2 52.4 %copy-start.42 = (f32[59]{0:T(128)S(1)}, f32[59]{0:T(128)}, u32[]{:S(2)}) copy-start(f32[59]{0:T(128)} %compare_select_fusion.7) | copy-start | bytes 712
  542.3 19.0 %copy-start.5 = (f32[59,4096]{1,0:T(8,128)S(1)}, f32[59,4096]{1,0:T(8,128)}, u32[]{:S(2)}) copy-start(f32[59,4096]{1,0:T(8,128)} %get-tuple-element.947) | copy-start | bytes 2899972
  542.3 57.6 %all-to-all-start.2 = ((f32[59,128,1]{0,2,1:T(1,128)}), f32[59,128,1]{0,2,1:T(1,128)S(1)}, u32[]{:S(2)}, u32[]{:S(2)}) async-start(f32[59,128,1]{0,2,1:T(1,128)} %bitcast.35), calls=%async_computation.2 | async-start | bytes 131072 | tf_op jit(solution)/shard_map/all_to_all | solution.py:254
  599.9 25.2 %all-to-all-start.3 = ((f32[59,128,1]{0,2,1:T(1,128)}), f32[59,128,1]{0,2,1:T(1,128)S(1)}, u32[]{:S(2)}, u32[]{:S(2)}) async-start(f32[59,128,1]{0,2,1:T(1,128)} %bitcast.39), calls=%async_computation.3 | async-start | bytes 131072 | tf_op jit(solution)/shard_map/all_to_all | solution.py:257
  625.1 17.3 %all-to-all-start.4 = ((f32[59,128,1]{0,2,1:T(1,128)}), f32[59,128,1]{0,2,1:T(1,128)S(1)}, u32[]{:S(2)}, u32[]{:S(2)}) async-start(f32[59,128,1]{0,2,1:T(1,128)} %bitcast.43), calls=%async_computation.4 | async-start | bytes 131072 | tf_op jit(solution)/shard_map/all_to_all | solution.py:258
  (25 other events, 79.9 us)
Sparse Core Ops, SparseCore 0:
  472.8 48.7 all-reduce.34
where the time goes:
time: 658 us; the launch traced here: 653 us
  local copies, waits for them, and re-layouts  193 us (29%)
  other arithmetic  191 us (29%)
  waiting for transfers between devices  100 us (15%)
  starting transfers between devices  62.2 us (9%)
  matrix products  45.8 us (7%)
  loops' own time  45.5 us (7%)
  between operations  14.6 us (2%)
    lt x64, other arithmetic, advance(): is_live = block_start + jnp.arange(BLOCK, dtype=jnp.int32) < list_count  79.8 us
    psum x1, waiting for transfers between devices, per_device(): gradient = lax.psum(view_grads, 'view')  48.9 us
    scatter-add x16, other arithmetic, one_tile(): return slot_grads.at[:, entries].add(feat_grads)  42.8 us
    another operation x1, loops' own time, per_device(): lax.fori_loop(0, tiles_here, one_tile, jnp.zeros((FEATS, arrived.shape[1]...  41.1 us
    dynamic_slice x96, local copies, waits for them, and re-layouts, render_blocks(): final_pair = lax.scan(block_step, start_pair, (in_blocks, block_starts))[0]  39.1 us
    dot_general x96, matrix products, advance(): jnp.dot(log_keep, triangle, precision=lax.Precision.HIGHEST)  26.8 us
    dynamic_slice x16, local copies, waits for them, and re-layouts, one_tile(): tile_id = tile_ids[0, tile_index]  21.1 us
    unnamed x95, local copies, waits for them, and re-layouts  20.8 us
  transfers between devices with their start and end apart: 6, of which 5 were waited for; matrix products, arithmetic and copies ran while one was open for 8% of the time, Pallas kernels for 0%

commit v1 on v0

v1 whole, which is shorter than its diff:
```python
import functools

import jax
import jax.numpy as jnp
from jax import lax
from jax.experimental import pallas as pl
from jax.experimental.pallas import tpu as pltpu
from jax.sharding import PartitionSpec as P

PARAMS = 59
PADDED = 64
FEATS = 9
LANES = 128
TILE_SIDE = 16
TILES_X = 64
ADAM_STEP = 1000
FOCAL_LEN = 1.2
DILATION = 0.3
SH_C0 = 0.28209479177387814
SH_C1 = 0.4886025119029199
SH_C2 = (
    1.0925484305920792,
    -1.0925484305920792,
    0.31539156525252005,
    -1.0925484305920792,
    0.5462742152960396,
)
SH_C3 = (
    -0.5900435899266435,
    2.890611442640554,
    -0.4570457994644658,
    0.3731763325901154,
    -0.4570457994644658,
    1.445305721320277,
    -0.5900435899266435,
)
BETA_ONE = 0.9
BETA_TWO = 0.999
ADAM_EPS = 1e-08
WIDTH = 1024.0
HEIGHT = 512.0


def sh_basis(x, y, z):
    xx, yy, zz = x * x, y * y, z * z
    return [
        SH_C0 + 0.0 * x,
        -SH_C1 * y,
        SH_C1 * z,
        -SH_C1 * x,
        SH_C2[0] * x * y,
        SH_C2[1] * y * z,
        SH_C2[2] * (2.0 * zz - xx - yy),
        SH_C2[3] * x * z,
        SH_C2[4] * (xx - yy),
        SH_C3[0] * y * (3.0 * xx - yy),
        SH_C3[1] * x * y * z,
        SH_C3[2] * y * (4.0 * zz - xx - yy),
        SH_C3[3] * z * (2.0 * zz - 3.0 * xx - 3.0 * yy),
        SH_C3[4] * x * (4.0 * zz - xx - yy),
        SH_C3[5] * z * (xx - yy),
        SH_C3[6] * x * (xx - 3.0 * yy),
    ]


def project(values, center):
    off = [values[i] - center[i] for i in range(3)]
    inverse = 1.0 / off[2]
    mean_u = 0.5 + FOCAL_LEN * off[0] * inverse
    mean_v = 0.5 + FOCAL_LEN * off[1] * inverse
    scale_sq = [jnp.exp(2.0 * values[3 + i]) for i in range(3)]
    quat = values[6:10]
    norm = lax.rsqrt(
        quat[0] * quat[0] + quat[1] * quat[1] + quat[2] * quat[2] + quat[3] * quat[3]
    )
    w, x, y, z = (q * norm for q in quat)
    rotation = [
        [1.0 - 2.0 * (y * y + z * z), 2.0 * (x * y - w * z), 2.0 * (x * z + w * y)],
        [2.0 * (x * y + w * z), 1.0 - 2.0 * (x * x + z * z), 2.0 * (y * z - w * x)],
        [2.0 * (x * z - w * y), 2.0 * (y * z + w * x), 1.0 - 2.0 * (x * x + y * y)],
    ]
    focal_now = FOCAL_LEN * inverse
    slope_u = -focal_now * off[0] * inverse
    slope_v = -focal_now * off[1] * inverse
    cov_uu = DILATION / (WIDTH * WIDTH)
    cov_vv = DILATION / (HEIGHT * HEIGHT)
    cov_uv = 0.0
    for c in range(3):
        axis_u = focal_now * rotation[0][c] + slope_u * rotation[2][c]
        axis_v = focal_now * rotation[1][c] + slope_v * rotation[2][c]
        cov_uu = cov_uu + axis_u * axis_u * scale_sq[c]
        cov_vv = cov_vv + axis_v * axis_v * scale_sq[c]
        cov_uv = cov_uv + axis_u * axis_v * scale_sq[c]
    inv_det = 1.0 / (cov_uu * cov_vv - cov_uv * cov_uv)
    inv_dist = 1.0 / jnp.sqrt(off[0] * off[0] + off[1] * off[1] + off[2] * off[2])
    basis = sh_basis(off[0] * inv_dist, off[1] * inv_dist, off[2] * inv_dist)
    colors = []
    for ch in range(3):
        total = basis[0] * values[11 + ch]
        for k in range(1, 16):
            total = total + basis[k] * values[11 + 3 * k + ch]
        colors.append(0.5 + total)
    opacity = 1.0 / (1.0 + jnp.exp(-values[10]))
    return [
        mean_u,
        mean_v,
        cov_vv * inv_det,
        -cov_uv * inv_det,
        cov_uu * inv_det,
        *colors,
        opacity,
    ]


def pick(array, index):
    return jnp.take_along_axis(array, index, axis=1, mode="promise_in_bounds")


def lane_ids(rows=8):
    return lax.broadcasted_iota(jnp.int32, (rows, LANES), 1)


def row_ids(rows=8):
    return lax.broadcasted_iota(jnp.int32, (rows, LANES), 0)


def fill_dense(array_ref, dense_ref):
    for j in range(32):
        dense_ref[PADDED * j : PADDED * j + PARAMS, :] = array_ref[
            :, LANES * j : LANES * (j + 1)
        ]


def dense_at(dense_ref, chunk, row):
    return dense_ref[pl.ds(chunk * 8 * PADDED + row, 8, stride=PADDED), :]


def project_kernel(center_ref, rows_ref, params_ref, out_ref, dense, feats):
    fill_dense(params_ref, dense)
    center = [center_ref[0, i] for i in range(3)]
    for chunk in range(4):
        values = [dense_at(dense, chunk, p) for p in range(PARAMS)]
        for f, value in enumerate(project(values, center)):
            feats[f, 8 * chunk : 8 * chunk + 8, :] = value
    rows = rows_ref[...]
    high = rows // LANES
    low = lax.rem(rows, LANES)
    slots = [jnp.zeros((8, LANES), jnp.float32)] * FEATS
    for h in range(32):
        chosen = high == h
        for f in range(FEATS):
            source = jnp.broadcast_to(feats[f, h : h + 1, :], (8, LANES))
            slots[f] = jnp.where(chosen, pick(source, low), slots[f])
    lane = lane_ids()
    sub = row_ids()
    for block in range(16):
        index = ((block % 2) * 8 + sub) * 8 + lax.rem(lane, 8)
        message = jnp.zeros((8, LANES), jnp.float32)
        for f in range(FEATS):
            source = jnp.broadcast_to(slots[f][block // 2 : block // 2 + 1, :], (8, LANES))
            message = jnp.where(lane // 8 == f, pick(source, index), message)
        out_ref[8 * block : 8 * block + 8, :] = message


def dot(a, b, dims=((1,), (0,))):
    return lax.dot_general(
        a,
        b,
        (dims, ((), ())),
        precision=lax.Precision.HIGHEST,
        preferred_element_type=jnp.float32,
    )


def render_kernel(
    arrived_ref,
    lists_ref,
    counts_ref,
    ids_ref,
    target_ref,
    out_ref,
    gauss,
    trans,
    gauss_grad,
    weight,
    sums,
):
    lane = lane_ids()
    sub = row_ids()
    half_of = lane // 64
    entry = lax.rem(lane, 64)
    slot = lax.rem(lists_ref[...], 64)
    from_owner = slot // 8
    within = lax.rem(slot, 8)
    feats = [jnp.zeros((8, LANES), jnp.float32)] * FEATS
    for h in range(2):
        for o in range(8):
            block = arrived_ref[pl.ds(8 * h + o, 8, stride=16), :]
            chosen = (from_owner == o) & (half_of == h)
            for f in range(FEATS):
                feats[f] = jnp.where(chosen, pick(block, 8 * f + within), feats[f])
    ids = ids_ref[...]
    center_u = (lax.rem(ids, TILES_X) * TILE_SIDE + TILE_SIDE // 2).astype(jnp.float32)
    center_v = (ids // TILES_X * TILE_SIDE + TILE_SIDE // 2).astype(jnp.float32)
    mean_u = feats[0] * WIDTH - center_u
    mean_v = feats[1] * HEIGHT - center_v
    quad_a = feats[2] * (-0.5 / (WIDTH * WIDTH))
    quad_b = feats[3] * (-1.0 / (WIDTH * HEIGHT))
    quad_c = feats[4] * (-0.5 / (HEIGHT * HEIGHT))
    active = entry < counts_ref[...]
    opacity = jnp.where(active, feats[8], 0.0)
    pixel_u = lax.rem(lane, 16).astype(jnp.float32) - 7.5
    pixel_v = [(lane // 16 + 8 * p).astype(jnp.float32) - 7.5 for p in range(2)]
    ahead = [mean_u, mean_v, quad_a, quad_b, quad_c, *feats[5:8], opacity]

    def forward(e, carried):
        through, acc, place = carried
        through, acc = list(through), list(acc)
        for h in range(2):
            index = jnp.full((8, LANES), h * 64, jnp.int32) + e
            m_u, m_v, q_a, q_b, q_c, c_0, c_1, c_2, alpha_max = (
                pick(array, index) for array in ahead
            )
            place = jnp.where((pick(slot, index) == entry) & (half_of == h), e, place)
            diff_u = pixel_u - m_u
            part = diff_u * q_b
            square = diff_u * diff_u * q_a
            for p in range(2):
                diff_v = pixel_v[p] - m_v
                bell = jnp.exp(square + diff_v * (part + q_c * diff_v))
                alpha = alpha_max * bell
                n = 2 * h + p
                before = through[n]
                gauss[e, n] = bell
                trans[e, n] = before
                share = alpha * before
                through[n] = before - share
                for ch, color in enumerate((c_0, c_1, c_2)):
                    acc[3 * n + ch] = acc[3 * n + ch] + color * share
        return tuple(through), tuple(acc), place

    zero = jnp.zeros((8, LANES), jnp.float32)
    _, acc, place = lax.fori_loop(
        0,
        64,
        forward,
        ((zero + 1.0,) * 4, (zero,) * 12, jnp.zeros((8, LANES), jnp.int32)),
    )
    residual = []
    for h in range(2):
        for p in range(2):
            for ch in range(3):
                wanted = target_ref[pl.ds(6 * h + 2 * ch + p, 8, stride=12), :]
                residual.append(acc[3 * (2 * h + p) + ch] - wanted)

    def backward(i, carried):
        e = 63 - i
        behind = list(carried)
        for h in range(2):
            index = jnp.full((8, LANES), h * 64, jnp.int32) + e
            c_0, c_1, c_2, alpha_max = (pick(array, index) for array in ahead[5:9])
            for p in range(2):
                n = 2 * h + p
                bell = gauss[e, n]
                before = trans[e, n]
                alpha = alpha_max * bell
                shade = (
                    c_0 * residual[3 * n] + c_1 * residual[3 * n + 1] + c_2 * residual[3 * n + 2]
                )
                gap = shade - behind[n]
                behind[n] = behind[n] + alpha * gap
                start = pl.multiple_of(512 * h + 8 * e, 8)
                gauss_grad[p, pl.ds(start, 8), :] = before * gap * bell
                weight[p, pl.ds(start, 8), :] = alpha * before
        return tuple(behind)

    lax.fori_loop(0, 64, backward, (zero,) * 4)

    pix = row_ids(LANES)
    col = lane_ids(LANES)
    for_moments, for_colors = [], []
    for p in range(2):
        u = lax.rem(pix, 16).astype(jnp.float32) - 7.5
        v = (pix // 16 + 8 * p).astype(jnp.float32) - 7.5
        powers = [jnp.ones_like(u), u, v, u * u, u * v, v * v]
        table = jnp.zeros_like(u)
        for m, power in enumerate(powers):
            table = jnp.where(col == m, power, table)
        for_moments.append(table)
        stacked = [zero]
        for ch in range(3):
            for h in range(2):
                stacked.append(residual[3 * (2 * h + p) + ch])
        stacked += [zero] * 9
        for_colors.append(jnp.concatenate(stacked, axis=0).T)

    for k in range(8):
        rows = pl.ds(k, LANES, stride=8)
        total = (
            dot(gauss_grad[0, rows, :], for_moments[0])
            + dot(gauss_grad[1, rows, :], for_moments[1])
            + dot(weight[0, rows, :], for_colors[0])
            + dot(weight[1, rows, :], for_colors[1])
        )
        sums[64 * k : 64 * k + 64, :] = total.T[0:64, :]

    s_0, s_u, s_v, s_uu, s_uv, s_vv = (sums[pl.ds(m, 8, stride=64), :] for m in range(6))
    d_colors = []
    for ch in range(3):
        even = sums[pl.ds(8 + 16 * ch, 8, stride=65), :]
        odd = sums[pl.ds(16 + 16 * ch, 8, stride=65), :]
        d_colors.append(jnp.where(half_of == 0, even, odd))
    m_u = opacity * (s_u - mean_u * s_0)
    m_v = opacity * (s_v - mean_v * s_0)
    m_uu = opacity * (s_uu - mean_u * (2.0 * s_u - mean_u * s_0))
    m_vv = opacity * (s_vv - mean_v * (2.0 * s_v - mean_v * s_0))
    m_uv = opacity * (s_uv - mean_u * s_v - mean_v * (s_u - mean_u * s_0))
    grads = [
        -WIDTH * (2.0 * quad_a * m_u + quad_b * m_v),
        -HEIGHT * (2.0 * quad_c * m_v + quad_b * m_u),
        (-0.5 / (WIDTH * WIDTH)) * m_uu,
        (-1.0 / (WIDTH * HEIGHT)) * m_uv,
        (-0.5 / (HEIGHT * HEIGHT)) * m_vv,
        *d_colors,
        jnp.where(active, s_0, 0.0),
    ]
    for h in range(2):
        for o in range(8):
            base = h * 64 + o * 8 + lax.rem(lane, 8)
            index = h * 64 + pick(place, base)
            message = zero
            for f in range(FEATS):
                message = jnp.where(lane // 8 == f, pick(grads[f], index), message)
            out_ref[pl.ds(8 * h + o, 8, stride=16), :] = message


def step_sizes(rows):
    return jnp.where(
        rows < 3,
        0.00016,
        jnp.where(
            rows < 6,
            0.005,
            jnp.where(
                rows < 10,
                0.001,
                jnp.where(rows < 11, 0.05, jnp.where(rows < 14, 0.0025, 0.000125)),
            ),
        ),
    )


def update_kernel(
    centers_ref,
    order_ref,
    rows_ref,
    returned_ref,
    params_ref,
    first_ref,
    second_ref,
    new_params_ref,
    new_first_ref,
    new_second_ref,
    leaving_ref,
    dense,
    grads,
    by_slot,
    staged,
    before,
    after,
):
    fill_dense(params_ref, dense)
    lane = lane_ids()
    place = jnp.zeros((PADDED, LANES), jnp.float32)
    sub_high = row_ids(32)
    sub_low = row_ids(LANES)
    lane_value = lane_ids(32).astype(jnp.float32)
    for i in range(32):
        rows = rows_ref[i : i + 1, :]
        hit = sub_high == jnp.broadcast_to(rows // LANES, (32, LANES))
        left = jnp.concatenate(
            [jnp.where(hit, float(i), 0.0), jnp.where(hit, lane_value, 0.0)], axis=0
        )
        right = jnp.where(
            sub_low == jnp.broadcast_to(lax.rem(rows, LANES), (LANES, LANES)), 1.0, 0.0
        )
        place = place + lax.dot_general(
            left.astype(jnp.bfloat16),
            right.astype(jnp.bfloat16),
            (((1,), (1,)), ((), ())),
            preferred_element_type=jnp.float32,
        )
    place_high = (place[0:32] + 0.5).astype(jnp.int32)
    place_low = (place[32:64] + 0.5).astype(jnp.int32)
    for view in range(4):
        values = [jnp.zeros((8, LANES), jnp.float32)] * FEATS
        for o in range(16):
            block = returned_ref[view, pl.ds(o, 8, stride=16), :]
            chosen = lane // 8 == o
            for f in range(FEATS):
                values[f] = jnp.where(chosen, pick(block, 8 * f + lax.rem(lane, 8)), values[f])
        for f in range(FEATS):
            by_slot[f, 8 * view : 8 * view + 8, :] = values[f]
    sizes = step_sizes(row_ids(PADDED)[0:PARAMS])
    for chunk in range(4):
        high = place_high[8 * chunk : 8 * chunk + 8]
        low = place_low[8 * chunk : 8 * chunk + 8]

        def collect(h, values):
            chosen = high == h
            return tuple(
                jnp.where(
                    chosen,
                    pick(jnp.broadcast_to(by_slot[f, pl.ds(h, 1), :], (8, LANES)), low),
                    values[f],
                )
                for f in range(FEATS)
            )

        feat_grads = lax.fori_loop(
            0, 32, collect, (jnp.zeros((8, LANES), jnp.float32),) * FEATS
        )
        view = high // 8
        center = []
        for i in range(3):
            at = jnp.zeros((8, LANES), jnp.float32)
            for v in range(4):
                at = jnp.where(view == v, centers_ref[v, i], at)
            center.append(at)
        values = [dense_at(dense, chunk, p) for p in range(PARAMS)]
        _, pull_back = jax.vjp(lambda *args: project(args, center), *values)
        for p, grad in enumerate(pull_back(list(feat_grads))):
            grads[pl.ds(chunk * 8 * PADDED + p, 8, stride=PADDED), :] = grad

    bias_one = 1.0 - BETA_ONE**ADAM_STEP
    bias_two = 1.0 - BETA_TWO**ADAM_STEP
    staged[...] = jnp.zeros_like(staged)

    def adam(j, carried):
        columns = pl.ds(pl.multiple_of(j * LANES, LANES), LANES)
        gradient = grads[pl.ds(pl.multiple_of(j * PADDED, PADDED), PADDED), :][0:PARAMS]
        new_one = BETA_ONE * first_ref[:, columns] + (1.0 - BETA_ONE) * gradient
        new_two = BETA_TWO * second_ref[:, columns] + (1.0 - BETA_TWO) * gradient * gradient
        updated = params_ref[:, columns] - sizes * (new_one / bias_one) / (
            jnp.sqrt(new_two / bias_two) + ADAM_EPS
        )
        staged[0:PARAMS, :] = updated
        staged[PADDED : PADDED + PARAMS, :] = new_one
        staged[2 * PADDED : 2 * PADDED + PARAMS, :] = new_two
        before[columns, 0:LANES] = staged[0:LANES, :].T
        before[columns, LANES : 2 * LANES] = staged[LANES : 2 * LANES, :].T
        return carried

    lax.fori_loop(0, 32, adam, 0)

    def move(t, carried):
        for u in range(16):
            row = order_ref[t * 16 + u]
            after[pl.ds(t * 16 + u, 1), :] = before[pl.ds(row, 1), :]
        return carried

    lax.fori_loop(0, 256, move, 0)
    leaving_ref[...] = after[3968:4096, :]
    for j in range(31):
        write_columns(
            after[LANES * j : LANES * (j + 1), :],
            slice(LANES * j, LANES * (j + 1)),
            new_params_ref,
            new_first_ref,
            new_second_ref,
        )


def write_columns(rows, columns, new_params_ref, new_first_ref, new_second_ref):
    both = rows[:, 0:LANES].T
    new_params_ref[:, columns] = both[0:PARAMS, :]
    new_first_ref[:, columns] = both[PADDED : PADDED + PARAMS, :]
    new_second_ref[:, columns] = rows[:, LANES : 2 * LANES].T[0:PARAMS, :]


def arrive_kernel(rows_ref, p_in, f_in, s_in, new_params_ref, new_first_ref, new_second_ref):
    del p_in, f_in, s_in
    write_columns(
        rows_ref[...], slice(0, LANES), new_params_ref, new_first_ref, new_second_ref
    )


VMEM = pl.BlockSpec(memory_space=pltpu.VMEM)
SMEM = pl.BlockSpec(memory_space=pltpu.SMEM)
WIDE = pltpu.CompilerParams(vmem_limit_bytes=48 * 1024 * 1024)


def f32(*shape):
    return jax.ShapeDtypeStruct(shape, jnp.float32)


def scratch(*shape):
    return pltpu.VMEM(shape, jnp.float32)


def per_device(
    params,
    first_moment,
    second_moment,
    cam_centers,
    target,
    send_rows,
    tile_lists,
    tile_counts,
    tile_ids,
    move_order,
):
    own_rows = send_rows.reshape(8, LANES)
    packed = jnp.concatenate(
        [own_rows.astype(jnp.float32), jnp.pad(cam_centers, ((0, 0), (0, LANES - 3)))], axis=0
    )
    packed_all = lax.all_gather(packed, "view")
    rows_all = packed_all[:, 0:8].reshape(32, LANES).astype(jnp.int32)
    centers_all = packed_all[:, 8, 0:3]

    outgoing = pl.pallas_call(
        project_kernel,
        out_shape=f32(LANES, LANES),
        in_specs=[SMEM, VMEM, VMEM],
        out_specs=VMEM,
        scratch_shapes=[scratch(32 * PADDED, LANES), scratch(FEATS, 32, LANES)],
        compiler_params=WIDE,
        name="project",
    )(cam_centers, own_rows, params)
    arrived = lax.all_to_all(outgoing, "dev", split_axis=0, concat_axis=0, tiled=True)

    def spread(array):
        return jnp.repeat(array.reshape(8, 2), 64, axis=1)

    slot_grads = pl.pallas_call(
        render_kernel,
        out_shape=f32(LANES, LANES),
        in_specs=[VMEM] * 5,
        out_specs=VMEM,
        scratch_shapes=[
            scratch(64, 4, 8, LANES),
            scratch(64, 4, 8, LANES),
            scratch(2, 1024, LANES),
            scratch(2, 1024, LANES),
            scratch(512, LANES),
        ],
        compiler_params=WIDE,
        name="render",
    )(
        arrived,
        tile_lists.reshape(8, LANES),
        spread(tile_counts),
        spread(tile_ids),
        target.reshape(96, LANES),
    )
    returned = lax.all_to_all(slot_grads, "dev", split_axis=0, concat_axis=0, tiled=True)
    returned_all = lax.all_gather(returned, "view")
    new_params, new_first, new_second, leaving = pl.pallas_call(
        update_kernel,
        out_shape=(f32(PARAMS, 4096),) * 3 + (f32(LANES, 2 * LANES),),
        in_specs=[SMEM, SMEM] + [VMEM] * 5,
        out_specs=(VMEM,) * 4,
        scratch_shapes=[
            scratch(32 * PADDED, LANES),
            scratch(32 * PADDED, LANES),
            scratch(FEATS, 32, LANES),
            scratch(2 * LANES, LANES),
            scratch(4096, 2 * LANES),
            scratch(4096, 2 * LANES),
        ],
        compiler_params=WIDE,
        name="update",
    )(
        centers_all,
        move_order.reshape(4096),
        rows_all,
        returned_all,
        params,
        first_moment,
        second_moment,
    )
    arriving = lax.all_to_all(leaving, "dev", split_axis=0, concat_axis=0, tiled=True)
    last = pl.BlockSpec((PARAMS, LANES), lambda i: (0, 31))
    whole = pl.BlockSpec(memory_space=pl.ANY)
    return pl.pallas_call(
        arrive_kernel,
        grid=(1,),
        out_shape=(f32(PARAMS, 4096),) * 3,
        in_specs=[pl.BlockSpec((LANES, 2 * LANES), lambda i: (0, 0)), whole, whole, whole],
        out_specs=(last,) * 3,
        input_output_aliases={1: 0, 2: 1, 3: 2},
        name="arrive",
    )(arriving, new_params, new_first, new_second)


def solution(mesh):
    placed = (
        P(None, "dev"),
        P(None, "dev"),
        P(None, "dev"),
        P("view", None),
        P("view", "dev", None, None),
        P("view", "dev", None),
        P("view", "dev", None),
        P("view", "dev"),
        P("view", "dev"),
        P("dev", None),
    )
    return jax.shard_map(
        per_device,
        mesh=mesh,
        in_specs=placed,
        out_specs=(P(None, "dev"), P(None, "dev"), P(None, "dev")),
        check_vma=False,
    )
```

time: 658 us -> 152 us (0.23)
  other arithmetic: 191 us -> 3.34 us
  local copies, waits for them, and re-layouts: 193 us -> 7.2 us
  waiting for transfers between devices: 100 us -> 11.4 us
  Pallas kernels: 0 us -> 54.4 us
  matrix products: 45.8 us -> 0 us
  loops' own time: 45.5 us -> 0 us
  blocking collectives: 0 us -> 39.5 us
  starting transfers between devices: 62.2 us -> 34.9 us
  between operations: 14.6 us -> 0.71 us
    lt x64 -> x0, other arithmetic: 79.8 us -> none  [advance(): is_live = block_start + jnp.arange(BLOCK, dtype=jnp.int32) < list_count]
    dynamic_slice x128 -> x0, local copies, waits for them, and re-layouts: 72.1 us -> none  [the longest x96 39.1 us: render_blocks(): final_pair = lax.scan(block_step, start_pair, (in_blocks, block_starts))[0]]
    gather x20 -> x0, local copies, waits for them, and re-layouts: 56.2 us -> none  [the longest x1 14.1 us: per_device(): ordered_params = updated[:, new_order]]
    pallas_call x0 -> x4, Pallas kernels: none -> 54.4 us  [the longest x1 35.1 us: per_device(): pl.pallas_call(update_kernel, out_shape=(f32(PARAMS, 4096),) * 3 + (f32(L...]
    scatter-add x17 -> x0, other arithmetic: 49.4 us -> none  [the longest x16 42.8 us: one_tile(): return slot_grads.at[:, entries].add(feat_grads)]
    psum x1 -> x0, waiting for transfers between devices: 48.9 us -> none  [per_device(): gradient = lax.psum(view_grads, 'view')]
    dot_general x192 -> x0, matrix products: 45.8 us -> none  [the longest x96 26.8 us: advance(): jnp.dot(log_keep, triangle, precision=lax.Precision.HIGHEST)]
    another operation x33 -> x0, loops' own time: 45.5 us -> none  [the longest x1 41.1 us: per_device(): lax.fori_loop(0, tiles_here, one_tile, jnp.zeros((FEATS, arrived.shape[1]...]
  transfers between devices with their start and end apart: 6 -> 2, of which waited for: 5 -> 1; matrix products, arithmetic and copies ran while one was open for 8% -> 4% of each run, Pallas kernels for 0% -> 0%
where the time goes in v1:
time: 152 us
  Pallas kernels  54.4 us (36%)
  blocking collectives  39.5 us (26%)
  starting transfers between devices  34.9 us (23%)
  waiting for transfers between devices  11.4 us (8%)
  local copies, waits for them, and re-layouts  7.2 us (5%)
  other arithmetic  3.34 us (2%)
    pallas_call x1, Pallas kernels, per_device(): pl.pallas_call(update_kernel, out_shape=(f32(PARAMS, 4096),) * 3 + (f32(L...  35.1 us
    all_to_all x1, blocking collectives, per_device(): lax.all_to_all(leaving, 'dev', split_axis=0, concat_axis=0, tiled=True)  20.2 us
    all_to_all x1, starting transfers between devices, per_device(): lax.all_to_all(outgoing, 'dev', split_axis=0, concat_axis=0, tiled=True)  18.4 us
    all_to_all x1, starting transfers between devices, per_device(): lax.all_to_all(slot_grads, 'dev', split_axis=0, concat_axis=0, tiled=True)  16.5 us
    pallas_call x1, Pallas kernels, per_device(): pl.pallas_call(render_kernel, out_shape=f32(LANES, LANES), in_specs=[VMEM...  15.3 us
    all_to_all x1, waiting for transfers between devices, per_device(): lax.all_to_all(slot_grads, 'dev', split_axis=0, concat_axis=0, tiled=True)  11.4 us
    all_gather x1, blocking collectives, per_device(): returned_all = lax.all_gather(returned, 'view')  9.84 us
    all_gather x1, blocking collectives, per_device(): packed_all = lax.all_gather(packed, 'view')  9.45 us
  transfers between devices with their start and end apart: 2, of which 1 were waited for; matrix products, arithmetic and copies ran while one was open for 4% of the time, Pallas kernels for 0%

profile of v1, /device:TPU:1, one launch (start us, length us, event | category | flops | bytes accessed | tf_op | source)
XLA Modules:
  0.0 151.5 jit_solution(18387172577858864755)
XLA Ops:
  0.6 0.6 copy-done.6
  1.3 1.2 copy-done
  2.5 0.7 copy-done.5
  3.2 2.3 %project.1 = f32[128,128]{1,0:T(8,128)} custom-call(f32[1,3]{1,0:T(1,128)S(1)} %copy-done.6, s32[8,128]{1,0:T(8,128)S(1)} %bitcast.24, f32[59,4096]{1,0:T(8,128)S(1)} %copy-done), custom_call_target="tpu_custom_call" | custom-call | tf_op jit(solution)/shard_map/project/pallas_call | solution.py:521
  5.5 18.4 %all-to-all-start = ((f32[128,1,128]{2,1,0:T(1,128)}), f32[128,1,128]{2,1,0:T(1,128)S(1)}, u32[]{:S(2)}, u32[]{:S(2)}) async-start(f32[128,1,128]{2,1,0:T(1,128)} %bitcast.6), calls=%async_computation | async-start | bytes 131072 | tf_op jit(solution)/shard_map/all_to_all | solution.py:530
  24.0 0.7 convert_element_type.10
  24.6 0.5 broadcast.12
  25.2 1.3 reduce.6
  26.5 1.3 reduce.7
  28.0 0.1 reshape.43.counts_ref
  28.2 0.1 reshape.45.ids_ref
  28.3 0.8 reshape.41.lists_ref
  29.1 9.4 %all-gather.2 = f32[4,9,128]{2,1,0:T(8,128)S(1)} all-gather(f32[1,9,128]{2,1,0:T(8,128)S(1)} %fusion.1), channel_id=2, replica_groups=mesh['view'=4,'dev'=128] {'view'}, dimensions={0}, use_global_device_ids=true | all-gather | bytes 23040 | tf_op jit(solution)/shard_map/all_gather | solution.py:517
  38.5 0.8 copy.23
  39.4 15.3 %render.1 = f32[128,128]{1,0:T(8,128)} custom-call(f32[128,128]{1,0:T(8,128)S(1)} %bitcast.20, s32[8,128]{1,0:T(8,128)S(1)} %reshape.41.lists_ref, s32[8,128]{1,0:T(8,128)S(1)} %reshape.43.counts_ref, s32[8,128]{1,0:T(8,128)S(1)} %reshape.45.ids_ref, f32[96,128]{1,0:T(8,128)S(1)} %reshape.46.target_ref), custom_call_target="tpu_custom_call" | custom-call | tf_op jit(solution)/shard_map/render/pallas_call | solution.py:535
  54.7 16.5 %all-to-all-start.1 = ((f32[128,1,128]{2,1,0:T(1,128)}), f32[128,1,128]{2,1,0:T(1,128)S(1)}, u32[]{:S(2)}, u32[]{:S(2)}) async-start(f32[128,1,128]{2,1,0:T(1,128)} %bitcast.9), calls=%async_computation.1 | async-start | bytes 131072 | tf_op jit(solution)/shard_map/all_to_all | solution.py:556
  71.3 11.4 %all-to-all-done.1 = f32[128,1,128]{2,1,0:T(1,128)S(1)} async-done(((f32[128,1,128]{2,1,0:T(1,128)}), f32[128,1,128]{2,1,0:T(1,128)S(1)}, u32[]{:S(2)}, u32[]{:S(2)}) %all-to-all-start.1) | async-done | bytes 65568 | tf_op jit(solution)/shard_map/all_to_all | solution.py:556
  82.7 9.8 %all-gather.1 = f32[512,1,128]{2,1,0:T(1,128)S(1)} all-gather(f32[128,1,128]{2,1,0:T(1,128)S(1)} %all-to-all-done.1), channel_id=3, replica_groups=mesh['view'=4,'dev'=128] {'view'}, dimensions={0}, use_global_device_ids=true | all-gather | bytes 327680 | tf_op jit(solution)/shard_map/all_gather | solution.py:557
  92.6 1.2 copy-done.3
  93.8 35.1 %update.1 = (f32[59,4096]{1,0:T(8,128)}, f32[59,4096]{1,0:T(8,128)}, f32[59,4096]{1,0:T(8,128)}, f32[128,256]{1,0:T(8,128)S(1)}) custom-call(f32[4,3]{1,0:T(4,128)S(1)} %bitcast.25, s32[4096]{0:T(1024)S(1)} %bitcast.22, s32[32,128]{1,0:T(8,128)S(1)} %fusion.rows_ref, f32[4,128,128]{2,1,0:T(8,128)S(1)} %bitcast.19, f32[59,4096]{1,0:T(8,128)S(1)} %copy-done.1, ...), custom_call_target="tpu_custom_call" | custom-call | tf_op jit(solution)/shard_map/update/pallas_call | solution.py:558
  128.9 0.1 copy.25
  129.0 20.2 %all_to_all.31 = f32[128,1,256]{2,1,0:T(1,128)S(1)} all-to-all(f32[128,1,256]{2,1,0:T(1,128)S(1)} %copy.25), channel_id=1, replica_groups=mesh['view'=4,'dev'=128] {'dev'}, dimensions={0} | all-to-all | bytes 262144 | tf_op jit(solution)/shard_map/all_to_all | solution.py:582
  149.2 0.7 copy.28
  149.9 1.6 %arrive.1 = (f32[59,4096]{1,0:T(8,128)}, f32[59,4096]{1,0:T(8,128)}, f32[59,4096]{1,0:T(8,128)}) custom-call(f32[128,256]{1,0:T(8,128)} %bitcast.26, f32[59,4096]{1,0:T(8,128)} %get-tuple-element.8.p_in, f32[59,4096]{1,0:T(8,128)} %get-tuple-element.9.f_in, f32[59,4096]{1,0:T(8,128)} %get-tuple-element.10.s_in), custom_call_target="tpu_custom_call", output_to_operand_aliasing={{0}: (1, {}), {1}: (2, {}), {2}: (3, {})} | custom-call | tf_op jit(solution)/shard_map/arrive/pallas_call | solution.py:585
  (19 shorter events, 0.4 us)
Async XLA Ops:
  0.6 0.7 copy-start.6
  1.3 1.2 copy-start
  2.5 0.7 copy-start.5
  3.2 89.3 %copy-start.1 = (f32[59,4096]{1,0:T(8,128)S(1)}, f32[59,4096]{1,0:T(8,128)}, u32[]{:S(2)}) copy-start(f32[59,4096]{1,0:T(8,128)} %params_ref.3) | copy-start | bytes 2899972
  3.2 89.3 %copy-start.2 = (f32[59,4096]{1,0:T(8,128)S(1)}, f32[59,4096]{1,0:T(8,128)}, u32[]{:S(2)}) copy-start(f32[59,4096]{1,0:T(8,128)} %first_ref.1) | copy-start | bytes 2899972
  5.5 33.9 %all-to-all-start = ((f32[128,1,128]{2,1,0:T(1,128)}), f32[128,1,128]{2,1,0:T(1,128)S(1)}, u32[]{:S(2)}, u32[]{:S(2)}) async-start(f32[128,1,128]{2,1,0:T(1,128)} %bitcast.6), calls=%async_computation | async-start | bytes 131072 | tf_op jit(solution)/shard_map/all_to_all | solution.py:530
  54.7 28.0 %all-to-all-start.1 = ((f32[128,1,128]{2,1,0:T(1,128)}), f32[128,1,128]{2,1,0:T(1,128)S(1)}, u32[]{:S(2)}, u32[]{:S(2)}) async-start(f32[128,1,128]{2,1,0:T(1,128)} %bitcast.9), calls=%async_computation.1 | async-start | bytes 131072 | tf_op jit(solution)/shard_map/all_to_all | solution.py:556
  82.7 9.8 %copy-start.4 = (s32[1,4096]{1,0:T(1,128)S(1)}, s32[1,4096]{1,0:T(1,128)}, u32[]{:S(2)}) copy-start(s32[1,4096]{1,0:T(1,128)} %param.19) | copy-start | bytes 49156
  92.5 1.2 copy-start.3

commit v2 on v1

--- a/solution.py
+++ b/solution.py
@@ -37,6 +37,7 @@
 BETA_ONE = 0.9
 BETA_TWO = 0.999
 ADAM_EPS = 1e-08
+MESH = pl.DeviceIdType.MESH
 WIDTH = 1024.0
 HEIGHT = 512.0
 
@@ -135,7 +136,77 @@
     return dense_ref[pl.ds(chunk * 8 * PADDED + row, 8, stride=PADDED), :]
 
 
-def project_kernel(center_ref, rows_ref, params_ref, out_ref, dense, feats):
+def greet(views, owners):
+    view, me = lax.axis_index("view"), lax.axis_index("dev")
+    barrier = pltpu.get_barrier_semaphore()
+    for i in range(1, views):
+        pl.semaphore_signal(
+            barrier, inc=1, device_id=(lax.rem(view + i, views), me), device_id_type=MESH
+        )
+
+    def signal(i, carried):
+        pl.semaphore_signal(
+            barrier, inc=1, device_id=(view, lax.rem(me + i, owners)), device_id_type=MESH
+        )
+        return carried
+
+    lax.fori_loop(1, owners, signal, 0)
+    return barrier, views + owners - 2
+
+
+def send_each(owners, message, landing, send_sem, recv_sem):
+    view, me = lax.axis_index("view"), lax.axis_index("dev")
+
+    def send(i, carried):
+        other = lax.rem(me + i, owners)
+        pltpu.make_async_remote_copy(
+            src_ref=message(other),
+            dst_ref=landing(me),
+            send_sem=send_sem,
+            recv_sem=recv_sem,
+            device_id=(view, other),
+            device_id_type=MESH,
+        ).start()
+        return carried
+
+    lax.fori_loop(1, owners, send, 0)
+
+
+def send_views(views, block, landing, send_sem, recv_sem):
+    view, me = lax.axis_index("view"), lax.axis_index("dev")
+    for i in range(1, views):
+        pltpu.make_async_remote_copy(
+            src_ref=block,
+            dst_ref=landing(view),
+            send_sem=send_sem,
+            recv_sem=recv_sem,
+            device_id=(lax.rem(view + i, views), me),
+            device_id_type=MESH,
+        ).start()
+
+
+def wait_bytes(ref, semaphore):
+    pltpu.make_async_copy(ref, ref, semaphore).wait()
+
+
+def project_kernel(
+    views,
+    owners,
+    center_ref,
+    packed_ref,
+    rows_ref,
+    params_ref,
+    arrived_ref,
+    packed_all_ref,
+    dense,
+    feats,
+    outgoing,
+    landed,
+    packed_landed,
+    sems,
+):
+    view, me = lax.axis_index("view"), lax.axis_index("dev")
+    barrier, expected = greet(views, owners)
     fill_dense(params_ref, dense)
     center = [center_ref[0, i] for i in range(3)]
     for chunk in range(4):
@@ -159,7 +230,25 @@
         for f in range(FEATS):
             source = jnp.broadcast_to(slots[f][block // 2 : block // 2 + 1, :], (8, LANES))
             message = jnp.where(lane // 8 == f, pick(source, index), message)
-        out_ref[8 * block : 8 * block + 8, :] = message
+        outgoing[8 * block : 8 * block + 8, :] = message
+    pl.semaphore_wait(barrier, expected)
+    send_each(
+        owners,
+        lambda d: outgoing.at[pl.ds(d, 1)],
+        lambda d: landed.at[pl.ds(d, 1)],
+        sems.at[0],
+        sems.at[1],
+    )
+    send_views(views, packed_ref, lambda v: packed_landed.at[v], sems.at[2], sems.at[3])
+    landed[pl.ds(me, 1), :] = outgoing[pl.ds(me, 1), :]
+    packed_landed[view] = packed_ref[...]
+    others = pl.ds(0, owners - 1)
+    wait_bytes(landed.at[others], sems.at[1])
+    wait_bytes(packed_landed.at[pl.ds(0, views - 1)], sems.at[3])
+    arrived_ref[...] = landed[...]
+    packed_all_ref[...] = packed_landed[...]
+    wait_bytes(landed.at[others], sems.at[0])
+    wait_bytes(packed_landed.at[pl.ds(0, views - 1)], sems.at[2])
 
 
 def dot(a, b, dims=((1,), (0,))):
@@ -172,7 +261,7 @@
     )
 
 
-def render_kernel(
+def render(
     arrived_ref,
     lists_ref,
     counts_ref,
@@ -245,6 +334,7 @@
         64,
         forward,
         ((zero + 1.0,) * 4, (zero,) * 12, jnp.zeros((8, LANES), jnp.int32)),
+        unroll=4,
     )
     residual = []
     for h in range(2):
@@ -274,7 +364,7 @@
                 weight[p, pl.ds(start, 8), :] = alpha * before
         return tuple(behind)
 
-    lax.fori_loop(0, 64, backward, (zero,) * 4)
+    lax.fori_loop(0, 64, backward, (zero,) * 4, unroll=4)
 
     pix = row_ids(LANES)
     col = lane_ids(LANES)
@@ -350,33 +440,13 @@
     )
 
 
-def update_kernel(
-    centers_ref,
-    order_ref,
-    rows_ref,
-    returned_ref,
-    params_ref,
-    first_ref,
-    second_ref,
-    new_params_ref,
-    new_first_ref,
-    new_second_ref,
-    leaving_ref,
-    dense,
-    grads,
-    by_slot,
-    staged,
-    before,
-    after,
-):
-    fill_dense(params_ref, dense)
-    lane = lane_ids()
+def slot_places(rows_all):
     place = jnp.zeros((PADDED, LANES), jnp.float32)
     sub_high = row_ids(32)
     sub_low = row_ids(LANES)
     lane_value = lane_ids(32).astype(jnp.float32)
     for i in range(32):
-        rows = rows_ref[i : i + 1, :]
+        rows = rows_all[i // 8][i % 8 : i % 8 + 1, :]
         hit = sub_high == jnp.broadcast_to(rows // LANES, (32, LANES))
         left = jnp.concatenate(
             [jnp.where(hit, float(i), 0.0), jnp.where(hit, lane_value, 0.0)], axis=0
@@ -390,51 +460,143 @@
             (((1,), (1,)), ((), ())),
             preferred_element_type=jnp.float32,
         )
-    place_high = (place[0:32] + 0.5).astype(jnp.int32)
-    place_low = (place[32:64] + 0.5).astype(jnp.int32)
-    for view in range(4):
-        values = [jnp.zeros((8, LANES), jnp.float32)] * FEATS
-        for o in range(16):
-            block = returned_ref[view, pl.ds(o, 8, stride=16), :]
-            chosen = lane // 8 == o
-            for f in range(FEATS):
-                values[f] = jnp.where(chosen, pick(block, 8 * f + lax.rem(lane, 8)), values[f])
+    return (place[0:32] + 0.5).astype(jnp.int32), (place[32:64] + 0.5).astype(jnp.int32)
+
+
+def step_kernel(
+    views,
+    owners,
+    order_ref,
+    packed_ref,
+    arrived_ref,
+    lists_ref,
+    counts_ref,
+    ids_ref,
+    target_ref,
+    params_hbm,
+    first_hbm,
+    second_hbm,
+    moved_a,
+    moved_b,
+    gauss,
+    trans,
+    gauss_grad,
+    weight,
+    sums,
+    params_ref,
+    first_ref,
+    second_ref,
+    slot_grads,
+    returned,
+    by_slot,
+    dense,
+    grads,
+    before_a,
+    before_b,
+    leaving,
+    arriving,
+    load_sems,
+    sems,
+):
+    view, me = lax.axis_index("view"), lax.axis_index("dev")
+    barrier, expected = greet(views, owners)
+    loads = [
+        pltpu.make_async_copy(source, place, load_sems.at[i])
+        for i, (source, place) in enumerate(
+            ((params_hbm, params_ref), (first_hbm, first_ref), (second_hbm, second_ref))
+        )
+    ]
+    for load in loads:
+        load.start()
+    lane = lane_ids()
+    place_high, place_low = slot_places(
+        [packed_ref[v, 0:8, :].astype(jnp.int32) for v in range(views)]
+    )
+    render(
+        arrived_ref,
+        lists_ref,
+        counts_ref,
+        ids_ref,
+        target_ref,
+        slot_grads,
+        gauss,
+        trans,
+        gauss_grad,
+        weight,
+        sums,
+    )
+    pl.semaphore_wait(barrier, expected)
+    send_each(
+        owners,
+        lambda d: slot_grads.at[pl.ds(d, 1)],
+        lambda d: returned.at[pl.ds(d, 1)],
+        sems.at[0],
+        sems.at[1],
+    )
+    returned[pl.ds(me, 1), :] = slot_grads[pl.ds(me, 1), :]
+    for load in loads:
+        load.wait()
+    fill_dense(params_ref, dense)
+    wait_bytes(returned.at[pl.ds(0, owners - 1)], sems.at[1])
+
+    values = [jnp.zeros((8, LANES), jnp.float32)] * FEATS
+    for o in range(16):
+        block = returned[pl.ds(o, 8, stride=16), :]
+        chosen = lane // 8 == o
         for f in range(FEATS):
-            by_slot[f, 8 * view : 8 * view + 8, :] = values[f]
+            values[f] = jnp.where(chosen, pick(block, 8 * f + lax.rem(lane, 8)), values[f])
+    for f in range(FEATS):
+        by_slot[view, 8 * f : 8 * f + 8, :] = values[f]
+    send_views(views, by_slot.at[view], lambda v: by_slot.at[v], sems.at[2], sems.at[3])
+    wait_bytes(by_slot.at[pl.ds(0, views - 1)], sems.at[3])
+
     sizes = step_sizes(row_ids(PADDED)[0:PARAMS])
-    for chunk in range(4):
-        high = place_high[8 * chunk : 8 * chunk + 8]
-        low = place_low[8 * chunk : 8 * chunk + 8]
-
-        def collect(h, values):
-            chosen = high == h
-            return tuple(
-                jnp.where(
-                    chosen,
-                    pick(jnp.broadcast_to(by_slot[f, pl.ds(h, 1), :], (8, LANES)), low),
-                    values[f],
-                )
-                for f in range(FEATS)
-            )
-
-        feat_grads = lax.fori_loop(
-            0, 32, collect, (jnp.zeros((8, LANES), jnp.float32),) * FEATS
-        )
-        view = high // 8
-        center = []
-        for i in range(3):
-            at = jnp.zeros((8, LANES), jnp.float32)
-            for v in range(4):
-                at = jnp.where(view == v, centers_ref[v, i], at)
-            center.append(at)
-        values = [dense_at(dense, chunk, p) for p in range(PARAMS)]
-        _, pull_back = jax.vjp(lambda *args: project(args, center), *values)
-        for p, grad in enumerate(pull_back(list(feat_grads))):
-            grads[pl.ds(chunk * 8 * PADDED + p, 8, stride=PADDED), :] = grad
+    for pair in range(2):
+        chunks = (2 * pair, 2 * pair + 1)
+        high = [place_high[8 * c : 8 * c + 8] for c in chunks]
+        low = [place_low[8 * c : 8 * c + 8] for c in chunks]
+        totals = ((jnp.zeros((8, LANES), jnp.float32),) * FEATS,) * 2
+        for v in range(views):
+
+            def collect(k, totals):
+                chosen = [h == 8 * v + k for h in high]
+                found = []
+                sources = [
+                    jnp.broadcast_to(by_slot[v, pl.ds(8 * f + k, 1), :], (8, LANES))
+                    for f in range(FEATS)
+                ]
+                for c in range(2):
+                    found.append(
+                        tuple(
+                            jnp.where(chosen[c], pick(sources[f], low[c]), totals[c][f])
+                            for f in range(FEATS)
+                        )
+                    )
+                return tuple(found)
+
+            totals = lax.fori_loop(0, 8, collect, totals, unroll=4)
+        for c in range(2):
+            chunk = chunks[c]
+            owner_view = high[c] // 8
+            center = []
+            for i in range(3):
+                at = jnp.zeros((8, LANES), jnp.float32)
+                for v in range(views):
+                    at = jnp.where(
+                        owner_view == v,
+                        jnp.broadcast_to(packed_ref[v, 8:9, i : i + 1], (8, LANES)),
+                        at,
+                    )
+                center.append(at)
+            arguments = [dense_at(dense, chunk, p) for p in range(PARAMS)]
+            _, pull_back = jax.vjp(lambda *args: project(args, center), *arguments)
+            for p, grad in enumerate(pull_back(list(totals[c]))):
+                grads[pl.ds(chunk * 8 * PADDED + p, 8, stride=PADDED), :] = grad
 
     bias_one = 1.0 - BETA_ONE**ADAM_STEP
     bias_two = 1.0 - BETA_TWO**ADAM_STEP
-    staged[...] = jnp.zeros_like(staged)
+    fill = jnp.zeros((PADDED - PARAMS, LANES), jnp.float32)
+    empty = jnp.zeros((PADDED, LANES), jnp.float32)
 
     def adam(j, carried):
         columns = pl.ds(pl.multiple_of(j * LANES, LANES), LANES)
@@ -444,50 +606,56 @@
         updated = params_ref[:, columns] - sizes * (new_one / bias_one) / (
             jnp.sqrt(new_two / bias_two) + ADAM_EPS
         )
-        staged[0:PARAMS, :] = updated
-        staged[PADDED : PADDED + PARAMS, :] = new_one
-        staged[2 * PADDED : 2 * PADDED + PARAMS, :] = new_two
-        before[columns, 0:LANES] = staged[0:LANES, :].T
-        before[columns, LANES : 2 * LANES] = staged[LANES : 2 * LANES, :].T
+        before_a[columns, :] = jnp.concatenate([updated, fill, new_one, fill], axis=0).T
+        before_b[columns, :] = jnp.concatenate([new_two, fill, empty], axis=0).T
         return carried
 
-    lax.fori_loop(0, 32, adam, 0)
+    lax.fori_loop(0, 32, adam, 0, unroll=4)
+
+    kept = order_ref.shape[0] - owners
+    for t in range(owners):
+        row = order_ref[kept + t]
+        leaving[0, t : t + 1, :] = before_a[pl.ds(row, 1), :]
+        leaving[1, t : t + 1, :] = before_b[pl.ds(row, 1), :]
+    send_each(
+        owners,
+        lambda d: leaving.at[:, pl.ds(d, 1)],
+        lambda d: arriving.at[:, pl.ds(d, 1)],
+        sems.at[4],
+        sems.at[5],
+    )
+    arriving[:, pl.ds(me, 1), :] = leaving[:, pl.ds(me, 1), :]
 
     def move(t, carried):
-        for u in range(16):
-            row = order_ref[t * 16 + u]
-            after[pl.ds(t * 16 + u, 1), :] = before[pl.ds(row, 1), :]
+        for u in range(32):
+            row = order_ref[t * 32 + u]
+            moved_a[pl.ds(t * 32 + u, 1), :] = before_a[pl.ds(row, 1), :]
+            moved_b[pl.ds(t * 32 + u, 1), :] = before_b[pl.ds(row, 1), :]
         return carried
 
-    lax.fori_loop(0, 256, move, 0)
-    leaving_ref[...] = after[3968:4096, :]
-    for j in range(31):
-        write_columns(
-            after[LANES * j : LANES * (j + 1), :],
-            slice(LANES * j, LANES * (j + 1)),
-            new_params_ref,
-            new_first_ref,
-            new_second_ref,
-        )
-
-
-def write_columns(rows, columns, new_params_ref, new_first_ref, new_second_ref):
-    both = rows[:, 0:LANES].T
-    new_params_ref[:, columns] = both[0:PARAMS, :]
-    new_first_ref[:, columns] = both[PADDED : PADDED + PARAMS, :]
-    new_second_ref[:, columns] = rows[:, LANES : 2 * LANES].T[0:PARAMS, :]
-
-
-def arrive_kernel(rows_ref, p_in, f_in, s_in, new_params_ref, new_first_ref, new_second_ref):
-    del p_in, f_in, s_in
-    write_columns(
-        rows_ref[...], slice(0, LANES), new_params_ref, new_first_ref, new_second_ref
-    )
+    lax.fori_loop(0, kept // 32, move, 0)
+    others = pl.ds(0, owners - 1)
+    wait_bytes(arriving.at[:, others], sems.at[5])
+    moved_a[kept:, :] = arriving[0]
+    moved_b[kept:, :] = arriving[1]
+    wait_bytes(returned.at[others], sems.at[0])
+    wait_bytes(by_slot.at[pl.ds(0, views - 1)], sems.at[2])
+    wait_bytes(arriving.at[:, others], sems.at[4])
+
+
+def write_kernel(moved_a, moved_b, new_params_ref, new_first_ref, new_second_ref):
+    for j in range(moved_a.shape[0] // LANES):
+        columns = slice(LANES * j, LANES * (j + 1))
+        both = moved_a[columns, :].T
+        new_params_ref[:, columns] = both[0:PARAMS, :]
+        new_first_ref[:, columns] = both[PADDED : PADDED + PARAMS, :]
+        new_second_ref[:, columns] = moved_b[columns, :].T[0:PARAMS, :]
 
 
 VMEM = pl.BlockSpec(memory_space=pltpu.VMEM)
 SMEM = pl.BlockSpec(memory_space=pltpu.SMEM)
-WIDE = pltpu.CompilerParams(vmem_limit_bytes=48 * 1024 * 1024)
+ANY = pl.BlockSpec(memory_space=pl.ANY)
+VMEM_BYTES = 48 * 1024 * 1024
 
 
 def f32(*shape):
@@ -510,87 +678,83 @@
     tile_ids,
     move_order,
 ):
+    views, owners = lax.axis_size("view"), lax.axis_size("dev")
     own_rows = send_rows.reshape(8, LANES)
     packed = jnp.concatenate(
-        [own_rows.astype(jnp.float32), jnp.pad(cam_centers, ((0, 0), (0, LANES - 3)))], axis=0
-    )
-    packed_all = lax.all_gather(packed, "view")
-    rows_all = packed_all[:, 0:8].reshape(32, LANES).astype(jnp.int32)
-    centers_all = packed_all[:, 8, 0:3]
-
-    outgoing = pl.pallas_call(
-        project_kernel,
-        out_shape=f32(LANES, LANES),
-        in_specs=[SMEM, VMEM, VMEM],
-        out_specs=VMEM,
-        scratch_shapes=[scratch(32 * PADDED, LANES), scratch(FEATS, 32, LANES)],
-        compiler_params=WIDE,
+        [own_rows.astype(jnp.float32), jnp.pad(cam_centers, ((0, 7), (0, LANES - 3)))], axis=0
+    )
+    arrived, packed_all = pl.pallas_call(
+        functools.partial(project_kernel, views, owners),
+        out_shape=(f32(owners, LANES), f32(views, 16, LANES)),
+        in_specs=[SMEM, VMEM, VMEM, VMEM],
+        out_specs=(VMEM, VMEM),
+        scratch_shapes=[
+            scratch(32 * PADDED, LANES),
+            scratch(FEATS, 32, LANES),
+            scratch(owners, LANES),
+            scratch(owners, LANES),
+            scratch(views, 16, LANES),
+            pltpu.SemaphoreType.DMA((4,)),
+        ],
+        compiler_params=pltpu.CompilerParams(
+            vmem_limit_bytes=VMEM_BYTES, collective_id=0, has_side_effects=True
+        ),
         name="project",
-    )(cam_centers, own_rows, params)
-    arrived = lax.all_to_all(outgoing, "dev", split_axis=0, concat_axis=0, tiled=True)
+    )(cam_centers, packed, own_rows, params)
 
     def spread(array):
         return jnp.repeat(array.reshape(8, 2), 64, axis=1)
 
-    slot_grads = pl.pallas_call(
-        render_kernel,
-        out_shape=f32(LANES, LANES),
-        in_specs=[VMEM] * 5,
-        out_specs=VMEM,
+    moved = pl.pallas_call(
+        functools.partial(step_kernel, views, owners),
+        out_shape=(f32(4096, LANES),) * 2,
+        in_specs=[SMEM] + [VMEM] * 6 + [ANY] * 3,
+        out_specs=(VMEM,) * 2,
         scratch_shapes=[
             scratch(64, 4, 8, LANES),
             scratch(64, 4, 8, LANES),
             scratch(2, 1024, LANES),
             scratch(2, 1024, LANES),
             scratch(512, LANES),
+            scratch(PARAMS, 4096),
+            scratch(PARAMS, 4096),
+            scratch(PARAMS, 4096),
+            scratch(owners, LANES),
+            scratch(owners, LANES),
+            scratch(views, 8 * FEATS, LANES),
+            scratch(32 * PADDED, LANES),
+            scratch(32 * PADDED, LANES),
+            scratch(4096, LANES),
+            scratch(4096, LANES),
+            scratch(2, owners, LANES),
+            scratch(2, owners, LANES),
+            pltpu.SemaphoreType.DMA((3,)),
+            pltpu.SemaphoreType.DMA((6,)),
         ],
-        compiler_params=WIDE,
-        name="render",
+        compiler_params=pltpu.CompilerParams(
+            vmem_limit_bytes=VMEM_BYTES, collective_id=1, has_side_effects=True
+        ),
+        name="step",
     )(
+        move_order.reshape(4096),
+        packed_all,
         arrived,
         tile_lists.reshape(8, LANES),
         spread(tile_counts),
         spread(tile_ids),
         target.reshape(96, LANES),
-    )
-    returned = lax.all_to_all(slot_grads, "dev", split_axis=0, concat_axis=0, tiled=True)
-    returned_all = lax.all_gather(returned, "view")
-    new_params, new_first, new_second, leaving = pl.pallas_call(
-        update_kernel,
-        out_shape=(f32(PARAMS, 4096),) * 3 + (f32(LANES, 2 * LANES),),
-        in_specs=[SMEM, SMEM] + [VMEM] * 5,
-        out_specs=(VMEM,) * 4,
-        scratch_shapes=[
-            scratch(32 * PADDED, LANES),
-            scratch(32 * PADDED, LANES),
-            scratch(FEATS, 32, LANES),
-            scratch(2 * LANES, LANES),
-            scratch(4096, 2 * LANES),
-            scratch(4096, 2 * LANES),
-        ],
-        compiler_params=WIDE,
-        name="update",
-    )(
-        centers_all,
-        move_order.reshape(4096),
-        rows_all,
-        returned_all,
         params,
         first_moment,
         second_moment,
     )
-    arriving = lax.all_to_all(leaving, "dev", split_axis=0, concat_axis=0, tiled=True)
-    last = pl.BlockSpec((PARAMS, LANES), lambda i: (0, 31))
-    whole = pl.BlockSpec(memory_space=pl.ANY)
     return pl.pallas_call(
-        arrive_kernel,
-        grid=(1,),
+        write_kernel,
+        grid=(4,),
         out_shape=(f32(PARAMS, 4096),) * 3,
-        in_specs=[pl.BlockSpec((LANES, 2 * LANES), lambda i: (0, 0)), whole, whole, whole],
-        out_specs=(last,) * 3,
-        input_output_aliases={1: 0, 2: 1, 3: 2},
-        name="arrive",
-    )(arriving, new_params, new_first, new_second)
+        in_specs=[pl.BlockSpec((1024, LANES), lambda i: (i, 0))] * 2,
+        out_specs=(pl.BlockSpec((PARAMS, 1024), lambda i: (0, i)),) * 3,
+        name="write",
+    )(*moved)
 
 
 def solution(mesh):

time: 152 us -> 87.2 us (0.57)
  blocking collectives: 39.5 us -> 0 us
  starting transfers between devices: 34.9 us -> 0 us
  Pallas kernels: 54.4 us -> 71 us
  waiting for transfers between devices: 11.4 us -> 0 us
  local copies, waits for them, and re-layouts: 7.2 us -> 10.9 us
    all_to_all x2 -> x0, starting transfers between devices: 34.9 us -> none  [the longest x1 18.4 us: per_device(): lax.all_to_all(outgoing, 'dev', split_axis=0, concat_axis=0, tiled=True)]
    all_to_all x1 -> x0, blocking collectives: 20.2 us -> none  [per_device(): lax.all_to_all(leaving, 'dev', split_axis=0, concat_axis=0, tiled=True)]
    all_gather x2 -> x0, blocking collectives: 19.3 us -> none  [the longest x1 9.84 us: per_device(): returned_all = lax.all_gather(returned, 'view')]
    pallas_call x4 -> x3, Pallas kernels: 54.4 us -> 71 us  [the longest x1 42.3 us: per_device(): pl.pallas_call(functools.partial(step_kernel, views, owners), out_shape=(...]
    all_to_all x2 -> x0, waiting for transfers between devices: 11.4 us -> none  [the longest x1 11.4 us: per_device(): lax.all_to_all(slot_grads, 'dev', split_axis=0, concat_axis=0, tiled=True)]
    unnamed x17 -> x18, local copies, waits for them, and re-layouts: 5.79 us -> 9.59 us
  transfers between devices with their start and end apart: 2 -> 0, of which waited for: 1 -> 0; matrix products, arithmetic and copies ran while one was open for 4% -> 0% of each run, Pallas kernels for 0% -> 0%
where the time goes in v2:
time: 87.2 us; the launch traced here: 86.6 us
  Pallas kernels  71 us (81%)
  local copies, waits for them, and re-layouts  10.9 us (12%)
  other arithmetic  4 us (5%)
    pallas_call x1, Pallas kernels, per_device(): pl.pallas_call(functools.partial(step_kernel, views, owners), out_shape=(...  42.3 us
    pallas_call x1, Pallas kernels, per_device(): pl.pallas_call(functools.partial(project_kernel, views, owners), out_shap...  23.8 us
    unnamed x18, local copies, waits for them, and re-layouts  9.59 us
    pallas_call x1, Pallas kernels, per_device(): pl.pallas_call(write_kernel, grid=(4,), out_shape=(f32(PARAMS, 4096),) *...  4.89 us
    unnamed x2, other arithmetic  2.64 us

profile of v2, /device:TPU:1, one launch (start us, length us, event | category | flops | bytes accessed | tf_op | source)
XLA Modules:
  0.0 86.6 jit_solution(8223344049910388654)
XLA Ops:
  0.6 0.5 broadcast.12
  1.1 1.3 %reduce.6 = s32[16]{0:T(128)S(1)} reduce(s32[1,16]{1,0:T(1,128)} %param.17, s32[]{:T(128)} %broadcast.12), dimensions={0}, to_apply=%param.17.reduce_sub_computation.3 | reduce | bytes 132 | tf_op args[7]
  2.5 1.3 %reduce.7 = s32[16]{0:T(128)S(1)} reduce(s32[1,16]{1,0:T(1,128)} %param.18, s32[]{:T(128)} %broadcast.12), dimensions={0}, to_apply=%param.18.reduce_sub_computation.3 | reduce | bytes 132 | tf_op args[8]
  3.8 0.1 reshape.35
  3.9 0.1 reshape.33
  3.9 0.1 broadcast_in_dim.6
  4.0 0.1 reshape.34.counts_ref
  4.1 0.1 broadcast_in_dim.7
  4.2 0.1 reshape.36.ids_ref
  4.2 0.7 convert_element_type.5
  5.0 0.7 select_maximum_fusion.packed_ref
  5.6 0.8 reshape.32.lists_ref
  6.4 0.8 copy.14
  7.3 1.2 %copy-done = f32[59,4096]{1,0:T(8,128)S(1)} copy-done((f32[59,4096]{1,0:T(8,128)S(1)}, f32[59,4096]{1,0:T(8,128)}, u32[]{:S(2)}) %copy-start) | copy-done | bytes 966680
  8.5 0.7 copy-done.6
  9.2 0.7 copy-done.7
  9.8 23.8 %project.1 = (f32[128,128]{1,0:T(8,128)S(1)}, f32[4,16,128]{2,1,0:T(8,128)S(1)}) custom-call(f32[1,3]{1,0:T(1,128)S(1)} %copy-done.7, f32[16,128]{1,0:T(8,128)S(1)} %select_maximum_fusion.packed_ref, s32[8,128]{1,0:T(8,128)S(1)} %bitcast.4, f32[59,4096]{1,0:T(8,128)S(1)} %copy-done), custom_call_target="tpu_custom_call" | custom-call | tf_op jit(solution)/shard_map/project/pallas_call | solution.py:686
  33.7 1.2 %copy-done.1 = f32[59,4096]{1,0:T(8,128)S(1)} copy-done((f32[59,4096]{1,0:T(8,128)S(1)}, f32[59,4096]{1,0:T(8,128)}, u32[]{:S(2)}) %copy-start.1) | copy-done | bytes 966680
  34.9 1.2 %copy-done.3 = f32[59,4096]{1,0:T(8,128)S(1)} copy-done((f32[59,4096]{1,0:T(8,128)S(1)}, f32[59,4096]{1,0:T(8,128)}, u32[]{:S(2)}) %copy-start.3) | copy-done | bytes 966680
  36.1 1.2 %copy-done.4 = f32[59,4096]{1,0:T(8,128)S(1)} copy-done((f32[59,4096]{1,0:T(8,128)S(1)}, f32[59,4096]{1,0:T(8,128)}, u32[]{:S(2)}) %copy-start.4) | copy-done | bytes 966680
  37.3 0.7 copy-done.5
  38.0 42.3 %step.1 = (f32[4096,128]{1,0:T(8,128)S(1)}, f32[4096,128]{1,0:T(8,128)}) custom-call(s32[4096]{0:T(1024)S(1)} %bitcast.2, f32[4,16,128]{2,1,0:T(8,128)S(1)} %get-tuple-element.7.packed_ref, f32[128,128]{1,0:T(8,128)S(1)} %get-tuple-element.8.arrived_ref, s32[8,128]{1,0:T(8,128)S(1)} %reshape.32.lists_ref, s32[8,128]{1,0:T(8,128)S(1)} %reshape.34.counts_ref, ...), custom_call_target="tpu_custom_call" | custom-call | tf_op jit(solution)/shard_map/step/pallas_call | solution.py:708
  80.4 1.3 %copy-done.2 = f32[4096,128]{1,0:T(8,128)} copy-done((f32[4096,128]{1,0:T(8,128)}, f32[4096,128]{1,0:T(8,128)S(1)}, u32[]{:S(2)}) %copy-start.2) | copy-done | bytes 2097176
  81.7 4.9 %write.1 = (f32[59,4096]{1,0:T(8,128)}, f32[59,4096]{1,0:T(8,128)}, f32[59,4096]{1,0:T(8,128)}) custom-call(f32[4096,128]{1,0:T(8,128)} %copy-done.2, f32[4096,128]{1,0:T(8,128)} %get-tuple-element.10.moved_b), custom_call_target="tpu_custom_call" | custom-call | tf_op jit(solution)/shard_map/write/pallas_call | solution.py:750
  (9 shorter events, 0.0 us)
Async XLA Ops:
  7.3 1.2 %copy-start = (f32[59,4096]{1,0:T(8,128)S(1)}, f32[59,4096]{1,0:T(8,128)}, u32[]{:S(2)}) copy-start(f32[59,4096]{1,0:T(8,128)} %params_hbm.1) | copy-start | bytes 2899972
  8.5 0.7 copy-start.6
  9.2 0.7 copy-start.7
  33.6 1.2 %copy-start.1 = (f32[59,4096]{1,0:T(8,128)S(1)}, f32[59,4096]{1,0:T(8,128)}, u32[]{:S(2)}) copy-start(f32[59,4096]{1,0:T(8,128)} %params_hbm.1) | copy-start | bytes 2899972
  34.9 1.2 %copy-start.3 = (f32[59,4096]{1,0:T(8,128)S(1)}, f32[59,4096]{1,0:T(8,128)}, u32[]{:S(2)}) copy-start(f32[59,4096]{1,0:T(8,128)} %first_hbm.1) | copy-start | bytes 2899972
  36.1 1.2 %copy-start.4 = (f32[59,4096]{1,0:T(8,128)S(1)}, f32[59,4096]{1,0:T(8,128)}, u32[]{:S(2)}) copy-start(f32[59,4096]{1,0:T(8,128)} %second_hbm.1) | copy-start | bytes 2899972
  37.3 0.7 copy-start.5
  80.4 1.3 %copy-start.2 = (f32[4096,128]{1,0:T(8,128)}, f32[4096,128]{1,0:T(8,128)S(1)}, u32[]{:S(2)}) copy-start(f32[4096,128]{1,0:T(8,128)S(1)} %get-tuple-element.9.moved_a) | copy-start | bytes 6291460

commit v3 on v2

--- a/solution.py
+++ b/solution.py
@@ -38,6 +38,7 @@
 BETA_TWO = 0.999
 ADAM_EPS = 1e-08
 MESH = pl.DeviceIdType.MESH
+MOVED_EARLY = 1984
 WIDTH = 1024.0
 HEIGHT = 512.0
 
@@ -189,31 +190,11 @@
     pltpu.make_async_copy(ref, ref, semaphore).wait()
 
 
-def project_kernel(
-    views,
-    owners,
-    center_ref,
-    packed_ref,
-    rows_ref,
-    params_ref,
-    arrived_ref,
-    packed_all_ref,
-    dense,
-    feats,
-    outgoing,
-    landed,
-    packed_landed,
-    sems,
-):
-    view, me = lax.axis_index("view"), lax.axis_index("dev")
-    barrier, expected = greet(views, owners)
-    fill_dense(params_ref, dense)
-    center = [center_ref[0, i] for i in range(3)]
+def slot_messages(rows, center, dense, feats, outgoing):
     for chunk in range(4):
         values = [dense_at(dense, chunk, p) for p in range(PARAMS)]
         for f, value in enumerate(project(values, center)):
             feats[f, 8 * chunk : 8 * chunk + 8, :] = value
-    rows = rows_ref[...]
     high = rows // LANES
     low = lax.rem(rows, LANES)
     slots = [jnp.zeros((8, LANES), jnp.float32)] * FEATS
@@ -231,24 +212,6 @@
             source = jnp.broadcast_to(slots[f][block // 2 : block // 2 + 1, :], (8, LANES))
             message = jnp.where(lane // 8 == f, pick(source, index), message)
         outgoing[8 * block : 8 * block + 8, :] = message
-    pl.semaphore_wait(barrier, expected)
-    send_each(
-        owners,
-        lambda d: outgoing.at[pl.ds(d, 1)],
-        lambda d: landed.at[pl.ds(d, 1)],
-        sems.at[0],
-        sems.at[1],
-    )
-    send_views(views, packed_ref, lambda v: packed_landed.at[v], sems.at[2], sems.at[3])
-    landed[pl.ds(me, 1), :] = outgoing[pl.ds(me, 1), :]
-    packed_landed[view] = packed_ref[...]
-    others = pl.ds(0, owners - 1)
-    wait_bytes(landed.at[others], sems.at[1])
-    wait_bytes(packed_landed.at[pl.ds(0, views - 1)], sems.at[3])
-    arrived_ref[...] = landed[...]
-    packed_all_ref[...] = packed_landed[...]
-    wait_bytes(landed.at[others], sems.at[0])
-    wait_bytes(packed_landed.at[pl.ds(0, views - 1)], sems.at[2])
 
 
 def dot(a, b, dims=((1,), (0,))):
@@ -263,10 +226,10 @@
 
 def render(
     arrived_ref,
-    lists_ref,
-    counts_ref,
-    ids_ref,
-    target_ref,
+    lists,
+    counts,
+    ids,
+    wanted_ref,
     out_ref,
     gauss,
     trans,
@@ -278,7 +241,7 @@
     sub = row_ids()
     half_of = lane // 64
     entry = lax.rem(lane, 64)
-    slot = lax.rem(lists_ref[...], 64)
+    slot = lax.rem(lists, 64)
     from_owner = slot // 8
     within = lax.rem(slot, 8)
     feats = [jnp.zeros((8, LANES), jnp.float32)] * FEATS
@@ -288,7 +251,6 @@
             chosen = (from_owner == o) & (half_of == h)
             for f in range(FEATS):
                 feats[f] = jnp.where(chosen, pick(block, 8 * f + within), feats[f])
-    ids = ids_ref[...]
     center_u = (lax.rem(ids, TILES_X) * TILE_SIDE + TILE_SIDE // 2).astype(jnp.float32)
     center_v = (ids // TILES_X * TILE_SIDE + TILE_SIDE // 2).astype(jnp.float32)
     mean_u = feats[0] * WIDTH - center_u
@@ -296,7 +258,7 @@
     quad_a = feats[2] * (-0.5 / (WIDTH * WIDTH))
     quad_b = feats[3] * (-1.0 / (WIDTH * HEIGHT))
     quad_c = feats[4] * (-0.5 / (HEIGHT * HEIGHT))
-    active = entry < counts_ref[...]
+    active = entry < counts
     opacity = jnp.where(active, feats[8], 0.0)
     pixel_u = lax.rem(lane, 16).astype(jnp.float32) - 7.5
     pixel_v = [(lane // 16 + 8 * p).astype(jnp.float32) - 7.5 for p in range(2)]
@@ -334,13 +296,13 @@
         64,
         forward,
         ((zero + 1.0,) * 4, (zero,) * 12, jnp.zeros((8, LANES), jnp.int32)),
-        unroll=4,
+        unroll=16,
     )
     residual = []
     for h in range(2):
         for p in range(2):
             for ch in range(3):
-                wanted = target_ref[pl.ds(6 * h + 2 * ch + p, 8, stride=12), :]
+                wanted = wanted_ref[pl.ds(16 * (2 * ch + p) + h, 8, stride=2), :]
                 residual.append(acc[3 * (2 * h + p) + ch] - wanted)
 
     def backward(i, carried):
@@ -364,7 +326,7 @@
                 weight[p, pl.ds(start, 8), :] = alpha * before
         return tuple(behind)
 
-    lax.fori_loop(0, 64, backward, (zero,) * 4, unroll=4)
+    lax.fori_loop(0, 64, backward, (zero,) * 4, unroll=16)
 
     pix = row_ids(LANES)
     col = lane_ids(LANES)
@@ -463,43 +425,64 @@
     return (place[0:32] + 0.5).astype(jnp.int32), (place[32:64] + 0.5).astype(jnp.int32)
 
 
+def per_tile(ref):
+    row, half_of = row_ids(), lane_ids() // 64
+    spread = jnp.zeros((8, LANES), jnp.int32)
+    for k in range(16):
+        spread = jnp.where((row == k // 2) & (half_of == k % 2), ref[0, k], spread)
+    return spread
+
+
 def step_kernel(
     views,
     owners,
+    center_ref,
     order_ref,
-    packed_ref,
-    arrived_ref,
-    lists_ref,
     counts_ref,
     ids_ref,
+    order_lanes_ref,
+    rows_ref,
+    lists_ref,
     target_ref,
     params_hbm,
     first_hbm,
     second_hbm,
+    new_params_ref,
+    new_first_ref,
+    new_second_ref,
+    params_ref,
+    first_ref,
+    second_ref,
+    dense,
+    feats,
+    outgoing,
+    landed,
+    packed,
+    packed_landed,
+    before_a,
+    before_b,
     moved_a,
     moved_b,
+    leaving,
+    arriving,
+    order_rows,
+    list_rows,
+    wanted,
     gauss,
     trans,
     gauss_grad,
     weight,
     sums,
-    params_ref,
-    first_ref,
-    second_ref,
     slot_grads,
     returned,
     by_slot,
-    dense,
+    leaving_grads,
+    arriving_grads,
     grads,
-    before_a,
-    before_b,
-    leaving,
-    arriving,
     load_sems,
     sems,
 ):
     view, me = lax.axis_index("view"), lax.axis_index("dev")
-    barrier, expected = greet(views, owners)
     loads = [
         pltpu.make_async_copy(source, place, load_sems.at[i])
         for i, (source, place) in enumerate(
@@ -508,113 +491,58 @@
     ]
     for load in loads:
         load.start()
+    barrier, expected = greet(views, owners)
     lane = lane_ids()
-    place_high, place_low = slot_places(
-        [packed_ref[v, 0:8, :].astype(jnp.int32) for v in range(views)]
-    )
-    render(
-        arrived_ref,
-        lists_ref,
-        counts_ref,
-        ids_ref,
-        target_ref,
-        slot_grads,
-        gauss,
-        trans,
-        gauss_grad,
-        weight,
-        sums,
-    )
+    others = pl.ds(0, owners - 1)
+    other_views = pl.ds(0, views - 1)
+    kept = order_ref.shape[1] - owners
+    zero = jnp.zeros((8, LANES), jnp.float32)
+
+    for i in range(8):
+        packed[i : i + 1, :] = rows_ref[0, :, LANES * i : LANES * (i + 1)].astype(jnp.float32)
+    here = zero
+    for i in range(3):
+        here = jnp.where(lane == i, center_ref[0, i], here)
+    packed[8:16, :] = here
+    loads[0].wait()
+    fill_dense(params_ref, dense)
+    slot_messages(
+        packed[0:8, :].astype(jnp.int32),
+        [center_ref[0, i] for i in range(3)],
+        dense,
+        feats,
+        outgoing,
+    )
+
+    fill = jnp.zeros((PADDED - PARAMS, LANES), jnp.float32)
+    empty = jnp.zeros((PADDED, LANES), jnp.float32)
+    loads[1].wait()
+    loads[2].wait()
+
+    def to_rows(j, carried):
+        columns = pl.ds(pl.multiple_of(j * LANES, LANES), LANES)
+        before_a[columns, :] = jnp.concatenate(
+            [params_ref[:, columns], fill, first_ref[:, columns], fill], axis=0
+        ).T
+        before_b[columns, :] = jnp.concatenate([second_ref[:, columns], fill, empty], axis=0).T
+        return carried
+
+    lax.fori_loop(0, 32, to_rows, 0, unroll=8)
+
     pl.semaphore_wait(barrier, expected)
     send_each(
         owners,
-        lambda d: slot_grads.at[pl.ds(d, 1)],
-        lambda d: returned.at[pl.ds(d, 1)],
+        lambda d: outgoing.at[pl.ds(d, 1)],
+        lambda d: landed.at[pl.ds(d, 1)],
         sems.at[0],
         sems.at[1],
     )
-    returned[pl.ds(me, 1), :] = slot_grads[pl.ds(me, 1), :]
-    for load in loads:
-        load.wait()
-    fill_dense(params_ref, dense)
-    wait_bytes(returned.at[pl.ds(0, owners - 1)], sems.at[1])
-
-    values = [jnp.zeros((8, LANES), jnp.float32)] * FEATS
-    for o in range(16):
-        block = returned[pl.ds(o, 8, stride=16), :]
-        chosen = lane // 8 == o
-        for f in range(FEATS):
-            values[f] = jnp.where(chosen, pick(block, 8 * f + lax.rem(lane, 8)), values[f])
-    for f in range(FEATS):
-        by_slot[view, 8 * f : 8 * f + 8, :] = values[f]
-    send_views(views, by_slot.at[view], lambda v: by_slot.at[v], sems.at[2], sems.at[3])
-    wait_bytes(by_slot.at[pl.ds(0, views - 1)], sems.at[3])
-
-    sizes = step_sizes(row_ids(PADDED)[0:PARAMS])
-    for pair in range(2):
-        chunks = (2 * pair, 2 * pair + 1)
-        high = [place_high[8 * c : 8 * c + 8] for c in chunks]
-        low = [place_low[8 * c : 8 * c + 8] for c in chunks]
-        totals = ((jnp.zeros((8, LANES), jnp.float32),) * FEATS,) * 2
-        for v in range(views):
-
-            def collect(k, totals):
-                chosen = [h == 8 * v + k for h in high]
-                found = []
-                sources = [
-                    jnp.broadcast_to(by_slot[v, pl.ds(8 * f + k, 1), :], (8, LANES))
-                    for f in range(FEATS)
-                ]
-                for c in range(2):
-                    found.append(
-                        tuple(
-                            jnp.where(chosen[c], pick(sources[f], low[c]), totals[c][f])
-                            for f in range(FEATS)
-                        )
-                    )
-                return tuple(found)
-
-            totals = lax.fori_loop(0, 8, collect, totals, unroll=4)
-        for c in range(2):
-            chunk = chunks[c]
-            owner_view = high[c] // 8
-            center = []
-            for i in range(3):
-                at = jnp.zeros((8, LANES), jnp.float32)
-                for v in range(views):
-                    at = jnp.where(
-                        owner_view == v,
-                        jnp.broadcast_to(packed_ref[v, 8:9, i : i + 1], (8, LANES)),
-                        at,
-                    )
-                center.append(at)
-            arguments = [dense_at(dense, chunk, p) for p in range(PARAMS)]
-            _, pull_back = jax.vjp(lambda *args: project(args, center), *arguments)
-            for p, grad in enumerate(pull_back(list(totals[c]))):
-                grads[pl.ds(chunk * 8 * PADDED + p, 8, stride=PADDED), :] = grad
-
-    bias_one = 1.0 - BETA_ONE**ADAM_STEP
-    bias_two = 1.0 - BETA_TWO**ADAM_STEP
-    fill = jnp.zeros((PADDED - PARAMS, LANES), jnp.float32)
-    empty = jnp.zeros((PADDED, LANES), jnp.float32)
-
-    def adam(j, carried):
-        columns = pl.ds(pl.multiple_of(j * LANES, LANES), LANES)
-        gradient = grads[pl.ds(pl.multiple_of(j * PADDED, PADDED), PADDED), :][0:PARAMS]
-        new_one = BETA_ONE * first_ref[:, columns] + (1.0 - BETA_ONE) * gradient
-        new_two = BETA_TWO * second_ref[:, columns] + (1.0 - BETA_TWO) * gradient * gradient
-        updated = params_ref[:, columns] - sizes * (new_one / bias_one) / (
-            jnp.sqrt(new_two / bias_two) + ADAM_EPS
-        )
-        before_a[columns, :] = jnp.concatenate([updated, fill, new_one, fill], axis=0).T
-        before_b[columns, :] = jnp.concatenate([new_two, fill, empty], axis=0).T
-        return carried
-
-    lax.fori_loop(0, 32, adam, 0, unroll=4)
-
-    kept = order_ref.shape[0] - owners
+    send_views(views, packed, lambda v: packed_landed.at[v], sems.at[2], sems.at[3])
+    landed[pl.ds(me, 1), :] = outgoing[pl.ds(me, 1), :]
+    packed_landed[view] = packed[...]
+
     for t in range(owners):
-        row = order_ref[kept + t]
+        row = order_ref[0, kept + t]
         leaving[0, t : t + 1, :] = before_a[pl.ds(row, 1), :]
         leaving[1, t : t + 1, :] = before_b[pl.ds(row, 1), :]
     send_each(
@@ -628,28 +556,165 @@
 
     def move(t, carried):
         for u in range(32):
-            row = order_ref[t * 32 + u]
+            row = order_ref[0, t * 32 + u]
             moved_a[pl.ds(t * 32 + u, 1), :] = before_a[pl.ds(row, 1), :]
             moved_b[pl.ds(t * 32 + u, 1), :] = before_b[pl.ds(row, 1), :]
         return carried
 
-    lax.fori_loop(0, kept // 32, move, 0)
-    others = pl.ds(0, owners - 1)
+    lax.fori_loop(0, MOVED_EARLY // 32, move, 0)
+    for k in range(16):
+        list_rows[k : k + 1, 0:64] = lists_ref[0, k : k + 1, :]
+    for ch in range(3):
+        for p in range(2):
+            n = 16 * (2 * ch + p)
+            wanted[n : n + 16, :] = target_ref[ch, :, LANES * p : LANES * (p + 1)]
+    even = list_rows[pl.ds(0, 8, stride=2), :]
+    odd = list_rows[pl.ds(1, 8, stride=2), :]
+    lists = jnp.where(lane < 64, even, pick(odd, lax.rem(lane, 64)))
+
+    wait_bytes(landed.at[others], sems.at[1])
+    render(
+        landed,
+        lists,
+        per_tile(counts_ref),
+        per_tile(ids_ref),
+        wanted,
+        slot_grads,
+        gauss,
+        trans,
+        gauss_grad,
+        weight,
+        sums,
+    )
+    send_each(
+        owners,
+        lambda d: slot_grads.at[pl.ds(d, 1)],
+        lambda d: returned.at[pl.ds(d, 1)],
+        sems.at[6],
+        sems.at[7],
+    )
+    returned[pl.ds(me, 1), :] = slot_grads[pl.ds(me, 1), :]
+
+    lax.fori_loop(MOVED_EARLY // 32, kept // 32, move, 0)
     wait_bytes(arriving.at[:, others], sems.at[5])
     moved_a[kept:, :] = arriving[0]
     moved_b[kept:, :] = arriving[1]
-    wait_bytes(returned.at[others], sems.at[0])
-    wait_bytes(by_slot.at[pl.ds(0, views - 1)], sems.at[2])
-    wait_bytes(arriving.at[:, others], sems.at[4])
-
-
-def write_kernel(moved_a, moved_b, new_params_ref, new_first_ref, new_second_ref):
-    for j in range(moved_a.shape[0] // LANES):
-        columns = slice(LANES * j, LANES * (j + 1))
+
+    def to_columns(j, carried):
+        columns = pl.ds(pl.multiple_of(j * LANES, LANES), LANES)
         both = moved_a[columns, :].T
         new_params_ref[:, columns] = both[0:PARAMS, :]
         new_first_ref[:, columns] = both[PADDED : PADDED + PARAMS, :]
         new_second_ref[:, columns] = moved_b[columns, :].T[0:PARAMS, :]
+        dense[pl.ds(pl.multiple_of(j * PADDED, PADDED), PADDED), :] = both[0:PADDED, :]
+        return carried
+
+    lax.fori_loop(0, 32, to_columns, 0, unroll=8)
+    for j in range(32):
+        order_rows[j : j + 1, :] = order_lanes_ref[:, LANES * j : LANES * (j + 1)]
+    wait_bytes(packed_landed.at[other_views], sems.at[3])
+    place_high, place_low = slot_places(
+        [packed_landed[v, 0:8, :].astype(jnp.int32) for v in range(views)]
+    )
+    place = place_high * LANES + place_low
+    slot_high, slot_low = [], []
+    for chunk in range(4):
+        order = order_rows[8 * chunk : 8 * chunk + 8, :]
+        high, low = order // LANES, lax.rem(order, LANES)
+        found = jnp.zeros((8, LANES), jnp.int32)
+        for h in range(32):
+            source = jnp.broadcast_to(place[h : h + 1, :], (8, LANES))
+            found = jnp.where(high == h, pick(source, low), found)
+        slot_high.append(found // LANES)
+        slot_low.append(lax.rem(found, LANES))
+    centers = [
+        [
+            jnp.broadcast_to(packed_landed[v, 8:9, i : i + 1], (8, LANES))
+            for v in range(views)
+        ]
+        for i in range(3)
+    ]
+
+    wait_bytes(returned.at[others], sems.at[7])
+    values = [zero] * FEATS
+    for o in range(16):
+        block = returned[pl.ds(o, 8, stride=16), :]
+        chosen = lane // 8 == o
+        for f in range(FEATS):
+            values[f] = jnp.where(chosen, pick(block, 8 * f + lax.rem(lane, 8)), values[f])
+    for f in range(FEATS):
+        by_slot[view, 8 * f : 8 * f + 8, :] = values[f]
+    send_views(views, by_slot.at[view], lambda v: by_slot.at[v], sems.at[8], sems.at[9])
+    wait_bytes(by_slot.at[other_views], sems.at[9])
+
+    def collect(chunk):
+        found = [zero] * FEATS
+        for h in range(32):
+            chosen = slot_high[chunk] == h
+            for f in range(FEATS):
+                row = 8 * f + h % 8
+                source = jnp.broadcast_to(by_slot[h // 8, row : row + 1, :], (8, LANES))
+                found[f] = jnp.where(chosen, pick(source, slot_low[chunk]), found[f])
+        return found
+
+    bias_one = 1.0 - BETA_ONE**ADAM_STEP
+    bias_two = 1.0 - BETA_TWO**ADAM_STEP
+    sizes = step_sizes(row_ids(PADDED)[0:PARAMS])
+
+    def finish(chunk, feat_grads, view_of):
+        center = []
+        for i in range(3):
+            at = zero
+            for v in range(views):
+                at = jnp.where(view_of == v, centers[i][v], at)
+            center.append(at)
+        arguments = [dense_at(dense, chunk, p) for p in range(PARAMS)]
+        _, pull_back = jax.vjp(lambda *args: project(args, center), *arguments)
+        for p, grad in enumerate(pull_back(list(feat_grads))):
+            grads[pl.ds(chunk * 8 * PADDED + p, 8, stride=PADDED), :] = grad
+        for j in range(8 * chunk, 8 * chunk + 8):
+            columns = slice(LANES * j, LANES * (j + 1))
+            gradient = grads[PADDED * j : PADDED * j + PARAMS, :]
+            new_one = BETA_ONE * new_first_ref[:, columns] + (1.0 - BETA_ONE) * gradient
+            new_two = BETA_TWO * new_second_ref[:, columns] + (1.0 - BETA_TWO) * gradient * gradient
+            new_params_ref[:, columns] = new_params_ref[:, columns] - sizes * (
+                new_one / bias_one
+            ) / (jnp.sqrt(new_two / bias_two) + ADAM_EPS)
+            new_first_ref[:, columns] = new_one
+            new_second_ref[:, columns] = new_two
+
+    last = collect(3)
+    last_view = slot_high[3] // 8
+    rows = [found[7:8, :] for found in last] + [last_view[7:8, :].astype(jnp.float32)]
+    rows.append(jnp.zeros((LANES - len(rows), LANES), jnp.float32))
+    leaving_grads[...] = jnp.concatenate(rows, axis=0).T
+    send_each(
+        owners,
+        lambda d: leaving_grads.at[pl.ds(d, 1)],
+        lambda d: arriving_grads.at[pl.ds(d, 1)],
+        sems.at[10],
+        sems.at[11],
+    )
+    arriving_grads[pl.ds(me, 1), :] = leaving_grads[pl.ds(me, 1), :]
+    for chunk in range(3):
+        finish(chunk, collect(chunk), slot_high[chunk] // 8)
+    wait_bytes(arriving_grads.at[others], sems.at[11])
+    arrived = arriving_grads[...].T
+    is_last = row_ids() == 7
+    last = [
+        jnp.where(is_last, jnp.broadcast_to(arrived[f : f + 1, :], (8, LANES)), last[f])
+        for f in range(FEATS)
+    ]
+    arrived_view = (arrived[FEATS : FEATS + 1, :] + 0.5).astype(jnp.int32)
+    finish(
+        3, last, jnp.where(is_last, jnp.broadcast_to(arrived_view, (8, LANES)), last_view)
+    )
+    wait_bytes(landed.at[others], sems.at[0])
+    wait_bytes(packed_landed.at[other_views], sems.at[2])
+    wait_bytes(arriving.at[:, others], sems.at[4])
+    wait_bytes(returned.at[others], sems.at[6])
+    wait_bytes(by_slot.at[other_views], sems.at[8])
+    wait_bytes(arriving_grads.at[others], sems.at[10])
 
 
 VMEM = pl.BlockSpec(memory_space=pltpu.VMEM)
@@ -679,82 +744,61 @@
     move_order,
 ):
     views, owners = lax.axis_size("view"), lax.axis_size("dev")
-    own_rows = send_rows.reshape(8, LANES)
-    packed = jnp.concatenate(
-        [own_rows.astype(jnp.float32), jnp.pad(cam_centers, ((0, 7), (0, LANES - 3)))], axis=0
-    )
-    arrived, packed_all = pl.pallas_call(
-        functools.partial(project_kernel, views, owners),
-        out_shape=(f32(owners, LANES), f32(views, 16, LANES)),
-        in_specs=[SMEM, VMEM, VMEM, VMEM],
-        out_specs=(VMEM, VMEM),
+    return pl.pallas_call(
+        functools.partial(step_kernel, views, owners),
+        out_shape=(f32(PARAMS, 4096),) * 3,
+        in_specs=[SMEM] * 4 + [VMEM] * 4 + [ANY] * 3,
+        out_specs=(VMEM,) * 3,
         scratch_shapes=[
+            scratch(PARAMS, 4096),
+            scratch(PARAMS, 4096),
+            scratch(PARAMS, 4096),
             scratch(32 * PADDED, LANES),
             scratch(FEATS, 32, LANES),
             scratch(owners, LANES),
             scratch(owners, LANES),
+            scratch(16, LANES),
             scratch(views, 16, LANES),
-            pltpu.SemaphoreType.DMA((4,)),
-        ],
-        compiler_params=pltpu.CompilerParams(
-            vmem_limit_bytes=VMEM_BYTES, collective_id=0, has_side_effects=True
-        ),
-        name="project",
-    )(cam_centers, packed, own_rows, params)
-
-    def spread(array):
-        return jnp.repeat(array.reshape(8, 2), 64, axis=1)
-
-    moved = pl.pallas_call(
-        functools.partial(step_kernel, views, owners),
-        out_shape=(f32(4096, LANES),) * 2,
-        in_specs=[SMEM] + [VMEM] * 6 + [ANY] * 3,
-        out_specs=(VMEM,) * 2,
-        scratch_shapes=[
+            scratch(4096, LANES),
+            scratch(4096, LANES),
+            scratch(4096, LANES),
+            scratch(4096, LANES),
+            scratch(2, owners, LANES),
+            scratch(2, owners, LANES),
+            pltpu.VMEM((32, LANES), jnp.int32),
+            pltpu.VMEM((16, LANES), jnp.int32),
+            scratch(96, LANES),
             scratch(64, 4, 8, LANES),
             scratch(64, 4, 8, LANES),
             scratch(2, 1024, LANES),
             scratch(2, 1024, LANES),
             scratch(512, LANES),
-            scratch(PARAMS, 4096),
-            scratch(PARAMS, 4096),
-            scratch(PARAMS, 4096),
             scratch(owners, LANES),
             scratch(owners, LANES),
             scratch(views, 8 * FEATS, LANES),
+            scratch(owners, LANES),
+            scratch(owners, LANES),
             scratch(32 * PADDED, LANES),
-            scratch(32 * PADDED, LANES),
-            scratch(4096, LANES),
-            scratch(4096, LANES),
-            scratch(2, owners, LANES),
-            scratch(2, owners, LANES),
             pltpu.SemaphoreType.DMA((3,)),
-            pltpu.SemaphoreType.DMA((6,)),
+            pltpu.SemaphoreType.DMA((12,)),
         ],
         compiler_params=pltpu.CompilerParams(
-            vmem_limit_bytes=VMEM_BYTES, collective_id=1, has_side_effects=True
+            vmem_limit_bytes=VMEM_BYTES, collective_id=0, has_side_effects=True
         ),
         name="step",
     )(
-        move_order.reshape(4096),
-        packed_all,
-        arrived,
-        tile_lists.reshape(8, LANES),
-        spread(tile_counts),
-        spread(tile_ids),
-        target.reshape(96, LANES),
+        cam_centers,
+        move_order,
+        tile_counts,
+        tile_ids,
+        move_order,
+        send_rows,
+        tile_lists,
+        target[0].transpose(1, 0, 2),
         params,
         first_moment,
         second_moment,
     )
-    return pl.pallas_call(
-        write_kernel,
-        grid=(4,),
-        out_shape=(f32(PARAMS, 4096),) * 3,
-        in_specs=[pl.BlockSpec((1024, LANES), lambda i: (i, 0))] * 2,
-        out_specs=(pl.BlockSpec((PARAMS, 1024), lambda i: (0, i)),) * 3,
-        name="write",
-    )(*moved)
 
 
 def solution(mesh):

time: 87.2 us -> 63 us (0.72)
  Pallas kernels: 71 us -> 53 us
  other arithmetic: 4 us -> 0 us
  local copies, waits for them, and re-layouts: 10.9 us -> 8.92 us
    pallas_call x2 -> x0, Pallas kernels: 28.7 us -> none  [the longest x1 23.8 us: per_device(): pl.pallas_call(functools.partial(project_kernel, views, owners), out_shap...]
    pallas_call x1, Pallas kernels: 42.3 us -> 53 us  [per_device(): pl.pallas_call(functools.partial(step_kernel, views, owners), out_shape=(...]
    unnamed x2 -> x0, other arithmetic: 2.64 us -> none
    reshape x6 -> x0, local copies, waits for them, and re-layouts: 1.12 us -> none  [the longest x1 0.77 us: per_device(): tile_lists.reshape(8, LANES)]
    unnamed x18 -> x21, local copies, waits for them, and re-layouts: 9.59 us -> 8.92 us
where the time goes in v3:
time: 63 us; the launch traced here: 62.6 us
  Pallas kernels  53 us (84%)
  local copies, waits for them, and re-layouts  8.92 us (14%)
  between operations  0.67 us (1%)
    pallas_call x1, Pallas kernels, per_device(): pl.pallas_call(functools.partial(step_kernel, views, owners), out_shape=(...  53 us
    unnamed x21, local copies, waits for them, and re-layouts  8.92 us

profile of v3, /device:TPU:1, one launch (start us, length us, event | category | flops | bytes accessed | tf_op | source)
XLA Modules:
  0.0 62.6 jit_solution(17107426611263288249)
XLA Ops:
  0.6 0.0 copy-start.8
  0.6 0.0 copy-start.7
  0.7 0.0 copy-start.6
  0.7 0.6 %copy-done.8 = s32[1,16]{1,0:T(1,128)S(1)} copy-done((s32[1,16]{1,0:T(1,128)S(1)}, s32[1,16]{1,0:T(1,128)}, u32[]{:S(2)}) %copy-start.8) | copy-done | bytes 88
  1.3 0.0 copy-done.7
  1.3 0.0 copy-done.6
  1.3 0.0 copy-start
  1.3 1.2 %copy-done = f32[59,4096]{1,0:T(8,128)S(1)} copy-done((f32[59,4096]{1,0:T(8,128)S(1)}, f32[59,4096]{1,0:T(8,128)}, u32[]{:S(2)}) %copy-start) | copy-done | bytes 966680
  2.5 0.0 copy-start.1
  2.5 1.2 %copy-done.1 = f32[59,4096]{1,0:T(8,128)S(1)} copy-done((f32[59,4096]{1,0:T(8,128)S(1)}, f32[59,4096]{1,0:T(8,128)}, u32[]{:S(2)}) %copy-start.1) | copy-done | bytes 966680
  3.8 0.0 copy-start.2
  3.8 0.7 %copy-done.2 = s32[1,4096]{1,0:T(1,128)S(1)} copy-done((s32[1,4096]{1,0:T(1,128)S(1)}, s32[1,4096]{1,0:T(1,128)}, u32[]{:S(2)}) %copy-start.2) | copy-done | bytes 16408
  4.5 0.0 copy-start.3
  4.5 0.8 %copy-done.3 = f32[1,16,3,256]{3,1,2,0:T(8,128)S(1)} copy-done((f32[1,16,3,256]{3,1,2,0:T(8,128)S(1)}, f32[1,16,3,256]{3,1,2,0:T(8,128)}, u32[]{:S(2)}) %copy-start.3) | copy-done | bytes 49176
  5.3 0.0 copy-start.4
  5.3 0.7 %copy-done.4 = s32[1,16,64]{2,1,0:T(8,128)S(1)} copy-done((s32[1,16,64]{2,1,0:T(8,128)S(1)}, s32[1,16,64]{2,1,0:T(8,128)}, u32[]{:S(2)}) %copy-start.4) | copy-done | bytes 4120
  6.0 0.0 copy-start.5
  6.0 0.7 %copy-done.5 = s32[1,1,1024]{2,1,0:T(1,128)S(1)} copy-done((s32[1,1,1024]{2,1,0:T(1,128)S(1)}, s32[1,1,1024]{2,1,0:T(1,128)}, u32[]{:S(2)}) %copy-start.5) | copy-done | bytes 4120
  6.7 53.0 %step.1 = (f32[59,4096]{1,0:T(8,128)S(1)}, f32[59,4096]{1,0:T(8,128)S(1)}, f32[59,4096]{1,0:T(8,128)S(1)}) custom-call(f32[1,3]{1,0:T(1,128)S(1)} %copy-done.6, s32[1,4096]{1,0:T(1,128)S(1)} %copy-done.2, s32[1,16]{1,0:T(1,128)S(1)} %copy-done.7, s32[1,16]{1,0:T(1,128)S(1)} %copy-done.8, s32[1,4096]{1,0:T(1,128)S(1)} %copy-done.2, ...), custom_call_target="tpu_custom_call" | custom-call | tf_op jit(solution)/shard_map/step/pallas_call | solution.py:747
  59.6 1.0 %copy.16 = f32[59,4096]{1,0:T(8,128)} copy(f32[59,4096]{1,0:T(8,128)S(1)} %get-tuple-element.6) | data formatting | bytes 1933312
  60.6 1.0 %copy.17 = f32[59,4096]{1,0:T(8,128)} copy(f32[59,4096]{1,0:T(8,128)S(1)} %get-tuple-element.7) | data formatting | bytes 1933312
  61.6 1.0 %copy.18 = f32[59,4096]{1,0:T(8,128)} copy(f32[59,4096]{1,0:T(8,128)S(1)} %get-tuple-element.8) | data formatting | bytes 1933312
Async XLA Ops:
  0.6 0.7 %copy-start.8 = (s32[1,16]{1,0:T(1,128)S(1)}, s32[1,16]{1,0:T(1,128)}, u32[]{:S(2)}) copy-start(s32[1,16]{1,0:T(1,128)} %ids_ref.1) | copy-start | bytes 196
  0.6 0.7 %copy-start.7 = (s32[1,16]{1,0:T(1,128)S(1)}, s32[1,16]{1,0:T(1,128)}, u32[]{:S(2)}) copy-start(s32[1,16]{1,0:T(1,128)} %counts_ref.1) | copy-start | bytes 196
  0.7 0.7 %copy-start.6 = (f32[1,3]{1,0:T(1,128)S(1)}, f32[1,3]{1,0:T(1,128)}, u32[]{:S(2)}) copy-start(f32[1,3]{1,0:T(1,128)} %center_ref.1) | copy-start | bytes 40
  1.3 1.2 %copy-start = (f32[59,4096]{1,0:T(8,128)S(1)}, f32[59,4096]{1,0:T(8,128)}, u32[]{:S(2)}) copy-start(f32[59,4096]{1,0:T(8,128)} %params_hbm.1) | copy-start | bytes 2899972
  2.5 1.2 %copy-start.1 = (f32[59,4096]{1,0:T(8,128)S(1)}, f32[59,4096]{1,0:T(8,128)}, u32[]{:S(2)}) copy-start(f32[59,4096]{1,0:T(8,128)} %first_hbm.1) | copy-start | bytes 2899972
  3.8 0.7 %copy-start.2 = (s32[1,4096]{1,0:T(1,128)S(1)}, s32[1,4096]{1,0:T(1,128)}, u32[]{:S(2)}) copy-start(s32[1,4096]{1,0:T(1,128)} %order_lanes_ref.1) | copy-start | bytes 49156
  4.5 0.8 %copy-start.3 = (f32[1,16,3,256]{3,1,2,0:T(8,128)S(1)}, f32[1,16,3,256]{3,1,2,0:T(8,128)}, u32[]{:S(2)}) copy-start(f32[1,16,3,256]{3,1,2,0:T(8,128)} %param.14) | copy-start | bytes 147460
  5.3 0.7 %copy-start.4 = (s32[1,16,64]{2,1,0:T(8,128)S(1)}, s32[1,16,64]{2,1,0:T(8,128)}, u32[]{:S(2)}) copy-start(s32[1,16,64]{2,1,0:T(8,128)} %lists_ref.1) | copy-start | bytes 12292
  6.0 0.7 %copy-start.5 = (s32[1,1,1024]{2,1,0:T(1,128)S(1)}, s32[1,1,1024]{2,1,0:T(1,128)}, u32[]{:S(2)}) copy-start(s32[1,1,1024]{2,1,0:T(1,128)} %rows_ref.1) | copy-start | bytes 12292

commit v4 on v3

--- a/solution.py
+++ b/solution.py
@@ -38,7 +38,7 @@
 BETA_TWO = 0.999
 ADAM_EPS = 1e-08
 MESH = pl.DeviceIdType.MESH
-MOVED_EARLY = 1984
+MOVED_EARLY = 2816
 WIDTH = 1024.0
 HEIGHT = 512.0
 
@@ -426,33 +426,45 @@
 
 
 def per_tile(ref):
+    values = ref[...]
     row, half_of = row_ids(), lane_ids() // 64
     spread = jnp.zeros((8, LANES), jnp.int32)
     for k in range(16):
-        spread = jnp.where((row == k // 2) & (half_of == k % 2), ref[0, k], spread)
+        one = jnp.broadcast_to(values[:, k : k + 1], (8, LANES))
+        spread = jnp.where((row == k // 2) & (half_of == k % 2), one, spread)
     return spread
 
 
 def step_kernel(
     views,
     owners,
-    center_ref,
-    order_ref,
-    counts_ref,
-    ids_ref,
-    order_lanes_ref,
-    rows_ref,
-    lists_ref,
-    target_ref,
     params_hbm,
     first_hbm,
     second_hbm,
+    center_hbm,
+    rows_hbm,
+    order_hbm,
+    lists_hbm,
+    target_hbm,
+    counts_hbm,
+    ids_hbm,
+    new_params_hbm,
+    new_first_hbm,
+    new_second_hbm,
     new_params_ref,
     new_first_ref,
     new_second_ref,
     params_ref,
     first_ref,
     second_ref,
+    center_ref,
+    rows_ref,
+    order_ref,
+    order_lanes_ref,
+    lists_ref,
+    target_ref,
+    counts_ref,
+    ids_ref,
     dense,
     feats,
     outgoing,
@@ -480,14 +492,26 @@
     arriving_grads,
     grads,
     load_sems,
+    store_sems,
     sems,
 ):
     view, me = lax.axis_index("view"), lax.axis_index("dev")
+    copies = (
+        (center_hbm, center_ref),
+        (rows_hbm, rows_ref),
+        (params_hbm, params_ref),
+        (first_hbm, first_ref),
+        (second_hbm, second_ref),
+        (order_hbm, order_ref),
+        (order_hbm, order_lanes_ref),
+        (lists_hbm, lists_ref),
+        (target_hbm, target_ref),
+        (counts_hbm, counts_ref),
+        (ids_hbm, ids_ref),
+    )
     loads = [
         pltpu.make_async_copy(source, place, load_sems.at[i])
-        for i, (source, place) in enumerate(
-            ((params_hbm, params_ref), (first_hbm, first_ref), (second_hbm, second_ref))
-        )
+        for i, (source, place) in enumerate(copies)
     ]
     for load in loads:
         load.start()
@@ -498,17 +522,19 @@
     kept = order_ref.shape[1] - owners
     zero = jnp.zeros((8, LANES), jnp.float32)
 
+    for load in loads[0:3]:
+        load.wait()
+    center = [jnp.broadcast_to(center_ref[:, i : i + 1], (8, LANES)) for i in range(3)]
     for i in range(8):
         packed[i : i + 1, :] = rows_ref[0, :, LANES * i : LANES * (i + 1)].astype(jnp.float32)
     here = zero
     for i in range(3):
-        here = jnp.where(lane == i, center_ref[0, i], here)
+        here = jnp.where(lane == i, center[i], here)
     packed[8:16, :] = here
-    loads[0].wait()
     fill_dense(params_ref, dense)
     slot_messages(
         packed[0:8, :].astype(jnp.int32),
-        [center_ref[0, i] for i in range(3)],
+        center,
         dense,
         feats,
         outgoing,
@@ -516,8 +542,8 @@
 
     fill = jnp.zeros((PADDED - PARAMS, LANES), jnp.float32)
     empty = jnp.zeros((PADDED, LANES), jnp.float32)
-    loads[1].wait()
-    loads[2].wait()
+    loads[3].wait()
+    loads[4].wait()
 
     def to_rows(j, carried):
         columns = pl.ds(pl.multiple_of(j * LANES, LANES), LANES)
@@ -529,6 +555,13 @@
 
     lax.fori_loop(0, 32, to_rows, 0, unroll=8)
 
+    for load in loads[5:]:
+        load.wait()
+    for t in range(owners):
+        row = order_ref[0, kept + t]
+        leaving[0, t : t + 1, :] = before_a[pl.ds(row, 1), :]
+        leaving[1, t : t + 1, :] = before_b[pl.ds(row, 1), :]
+
     pl.semaphore_wait(barrier, expected)
     send_each(
         owners,
@@ -541,10 +574,6 @@
     landed[pl.ds(me, 1), :] = outgoing[pl.ds(me, 1), :]
     packed_landed[view] = packed[...]
 
-    for t in range(owners):
-        row = order_ref[0, kept + t]
-        leaving[0, t : t + 1, :] = before_a[pl.ds(row, 1), :]
-        leaving[1, t : t + 1, :] = before_b[pl.ds(row, 1), :]
     send_each(
         owners,
         lambda d: leaving.at[:, pl.ds(d, 1)],
@@ -610,6 +639,17 @@
         return carried
 
     lax.fori_loop(0, 32, to_columns, 0, unroll=8)
+    wait_bytes(returned.at[others], sems.at[7])
+    values = [zero] * FEATS
+    for o in range(16):
+        block = returned[pl.ds(o, 8, stride=16), :]
+        chosen = lane // 8 == o
+        for f in range(FEATS):
+            values[f] = jnp.where(chosen, pick(block, 8 * f + lax.rem(lane, 8)), values[f])
+    for f in range(FEATS):
+        by_slot[view, 8 * f : 8 * f + 8, :] = values[f]
+    send_views(views, by_slot.at[view], lambda v: by_slot.at[v], sems.at[8], sems.at[9])
+
     for j in range(32):
         order_rows[j : j + 1, :] = order_lanes_ref[:, LANES * j : LANES * (j + 1)]
     wait_bytes(packed_landed.at[other_views], sems.at[3])
@@ -635,16 +675,6 @@
         for i in range(3)
     ]
 
-    wait_bytes(returned.at[others], sems.at[7])
-    values = [zero] * FEATS
-    for o in range(16):
-        block = returned[pl.ds(o, 8, stride=16), :]
-        chosen = lane // 8 == o
-        for f in range(FEATS):
-            values[f] = jnp.where(chosen, pick(block, 8 * f + lax.rem(lane, 8)), values[f])
-    for f in range(FEATS):
-        by_slot[view, 8 * f : 8 * f + 8, :] = values[f]
-    send_views(views, by_slot.at[view], lambda v: by_slot.at[v], sems.at[8], sems.at[9])
     wait_bytes(by_slot.at[other_views], sems.at[9])
 
     def collect(chunk):
@@ -660,6 +690,8 @@
     bias_one = 1.0 - BETA_ONE**ADAM_STEP
     bias_two = 1.0 - BETA_TWO**ADAM_STEP
     sizes = step_sizes(row_ids(PADDED)[0:PARAMS])
+
+    stores = []
 
     def finish(chunk, feat_grads, view_of):
         center = []
@@ -682,6 +714,19 @@
             ) / (jnp.sqrt(new_two / bias_two) + ADAM_EPS)
             new_first_ref[:, columns] = new_one
             new_second_ref[:, columns] = new_two
+        columns = pl.ds(8 * LANES * chunk, 8 * LANES)
+        for i, (source, place) in enumerate(
+            (
+                (new_params_ref, new_params_hbm),
+                (new_first_ref, new_first_hbm),
+                (new_second_ref, new_second_hbm),
+            )
+        ):
+            copy = pltpu.make_async_copy(
+                source.at[:, columns], place.at[:, columns], store_sems.at[3 * chunk + i]
+            )
+            copy.start()
+            stores.append(copy)
 
     last = collect(3)
     last_view = slot_high[3] // 8
@@ -715,12 +760,37 @@
     wait_bytes(returned.at[others], sems.at[6])
     wait_bytes(by_slot.at[other_views], sems.at[8])
     wait_bytes(arriving_grads.at[others], sems.at[10])
+    for copy in stores:
+        copy.wait()
+
+
+def write_kernel(
+    params, first, second, new_params, new_first, new_second, held, load_sems, store_sems
+):
+    loads, stores = [], []
+    for i, (source, place) in enumerate(
+        ((params, new_params), (first, new_first), (second, new_second))
+    ):
+        for part in range(4):
+            columns = pl.ds(1024 * part, 1024)
+            n = len(loads)
+            middle = held.at[i, :, columns]
+            loads.append(pltpu.make_async_copy(source.at[:, columns], middle, load_sems.at[n]))
+            stores.append(pltpu.make_async_copy(middle, place.at[:, columns], store_sems.at[n]))
+    for load in loads:
+        load.start()
+    for load, store in zip(loads, stores):
+        load.wait()
+        store.start()
+    for store in stores:
+        store.wait()
 
 
 VMEM = pl.BlockSpec(memory_space=pltpu.VMEM)
 SMEM = pl.BlockSpec(memory_space=pltpu.SMEM)
 ANY = pl.BlockSpec(memory_space=pl.ANY)
-VMEM_BYTES = 48 * 1024 * 1024
+HBM = pl.BlockSpec(memory_space=pltpu.HBM)
+VMEM_BYTES = 60 * 1024 * 1024
 
 
 def f32(*shape):
@@ -744,15 +814,27 @@
     move_order,
 ):
     views, owners = lax.axis_size("view"), lax.axis_size("dev")
-    return pl.pallas_call(
+    by_channel = target[0].transpose(1, 0, 2)
+    updated = pl.pallas_call(
         functools.partial(step_kernel, views, owners),
         out_shape=(f32(PARAMS, 4096),) * 3,
-        in_specs=[SMEM] * 4 + [VMEM] * 4 + [ANY] * 3,
-        out_specs=(VMEM,) * 3,
+        in_specs=[HBM] * 10,
+        out_specs=(ANY,) * 3,
         scratch_shapes=[
             scratch(PARAMS, 4096),
             scratch(PARAMS, 4096),
             scratch(PARAMS, 4096),
+            scratch(PARAMS, 4096),
+            scratch(PARAMS, 4096),
+            scratch(PARAMS, 4096),
+            scratch(*cam_centers.shape),
+            pltpu.VMEM(send_rows.shape, jnp.int32),
+            pltpu.SMEM(move_order.shape, jnp.int32),
+            pltpu.VMEM(move_order.shape, jnp.int32),
+            pltpu.VMEM(tile_lists.shape, jnp.int32),
+            scratch(*by_channel.shape),
+            pltpu.VMEM(tile_counts.shape, jnp.int32),
+            pltpu.VMEM(tile_ids.shape, jnp.int32),
             scratch(32 * PADDED, LANES),
             scratch(FEATS, 32, LANES),
             scratch(owners, LANES),
@@ -779,7 +861,8 @@
             scratch(owners, LANES),
             scratch(owners, LANES),
             scratch(32 * PADDED, LANES),
-            pltpu.SemaphoreType.DMA((3,)),
+            pltpu.SemaphoreType.DMA((11,)),
+            pltpu.SemaphoreType.DMA((12,)),
             pltpu.SemaphoreType.DMA((12,)),
         ],
         compiler_params=pltpu.CompilerParams(
@@ -787,18 +870,30 @@
         ),
         name="step",
     )(
-        cam_centers,
-        move_order,
-        tile_counts,
-        tile_ids,
-        move_order,
-        send_rows,
-        tile_lists,
-        target[0].transpose(1, 0, 2),
         params,
         first_moment,
         second_moment,
-    )
+        cam_centers,
+        send_rows,
+        move_order,
+        tile_lists,
+        by_channel,
+        tile_counts,
+        tile_ids,
+    )
+    return pl.pallas_call(
+        write_kernel,
+        out_shape=(f32(PARAMS, 4096),) * 3,
+        in_specs=[ANY] * 3,
+        out_specs=(HBM,) * 3,
+        scratch_shapes=[
+            scratch(3, PARAMS, 4096),
+            pltpu.SemaphoreType.DMA((12,)),
+            pltpu.SemaphoreType.DMA((12,)),
+        ],
+        compiler_params=pltpu.CompilerParams(vmem_limit_bytes=VMEM_BYTES),
+        name="write",
+    )(*updated)
 
 
 def solution(mesh):

time: 63 us -> 56.8 us (0.902)
  local copies, waits for them, and re-layouts: 8.92 us -> 0 us
  Pallas kernels: 53 us -> 56 us
    unnamed x21 -> x0, local copies, waits for them, and re-layouts: 8.92 us -> none
    pallas_call x0 -> x1, Pallas kernels: none -> 2.81 us  [per_device(): pl.pallas_call(write_kernel, out_shape=(f32(PARAMS, 4096),) * 3, in_specs...]
where the time goes in v4:
time: 56.8 us; the launch traced here: 56.7 us
  Pallas kernels  56 us (99%)
  between operations  0.64 us (1%)
    pallas_call x1, Pallas kernels, per_device(): pl.pallas_call(functools.partial(step_kernel, views, owners), out_shape=(...  53.2 us
    pallas_call x1, Pallas kernels, per_device(): pl.pallas_call(write_kernel, out_shape=(f32(PARAMS, 4096),) * 3, in_specs...  2.81 us

profile of v4, /device:TPU:1, one launch (start us, length us, event | category | flops | bytes accessed | tf_op | source)
XLA Modules:
  0.0 56.7 jit_solution(17821404561582121515)
XLA Ops:
  0.6 53.2 %step.1 = (f32[59,4096]{1,0:T(8,128)}, f32[59,4096]{1,0:T(8,128)}, f32[59,4096]{1,0:T(8,128)}) custom-call(f32[59,4096]{1,0:T(8,128)} %params_hbm.1, f32[59,4096]{1,0:T(8,128)} %first_hbm.1, f32[59,4096]{1,0:T(8,128)} %second_hbm.1, f32[1,3]{1,0:T(1,128)} %center_hbm.1, s32[1,1,1024]{2,1,0:T(1,128)} %rows_hbm.1, s32[1,4096]{1,0:T(1,128)} %order_hbm.1, ...), custom_call_target="tpu_custom_call" | custom-call | tf_op jit(solution)/shard_map/step/pallas_call | solution.py:818
  53.8 2.8 %write.1 = (f32[59,4096]{1,0:T(8,128)}, f32[59,4096]{1,0:T(8,128)}, f32[59,4096]{1,0:T(8,128)}) custom-call(f32[59,4096]{1,0:T(8,128)} %get-tuple-element.6.params, f32[59,4096]{1,0:T(8,128)} %get-tuple-element.7.first, f32[59,4096]{1,0:T(8,128)} %get-tuple-element.8.second), custom_call_target="tpu_custom_call" | custom-call | tf_op jit(solution)/shard_map/write/pallas_call | solution.py:884

commit v5 on v4

--- a/solution.py
+++ b/solution.py
@@ -137,6 +137,15 @@
     return dense_ref[pl.ds(chunk * 8 * PADDED + row, 8, stride=PADDED), :]
 
 
+def for_others(owners, body):
+    def step(i, carried):
+        body(i)
+        return carried
+
+    for low, high in ((40, 88), (24, 40), (88, 104), (1, 24), (104, 128)):
+        lax.fori_loop(low * owners // 128, high * owners // 128, step, 0, unroll=8)
+
+
 def greet(views, owners):
     view, me = lax.axis_index("view"), lax.axis_index("dev")
     barrier = pltpu.get_barrier_semaphore()
@@ -145,20 +154,19 @@
             barrier, inc=1, device_id=(lax.rem(view + i, views), me), device_id_type=MESH
         )
 
-    def signal(i, carried):
+    def signal(i):
         pl.semaphore_signal(
             barrier, inc=1, device_id=(view, lax.rem(me + i, owners)), device_id_type=MESH
         )
-        return carried
-
-    lax.fori_loop(1, owners, signal, 0)
+
+    for_others(owners, signal)
     return barrier, views + owners - 2
 
 
 def send_each(owners, message, landing, send_sem, recv_sem):
     view, me = lax.axis_index("view"), lax.axis_index("dev")
 
-    def send(i, carried):
+    def send(i):
         other = lax.rem(me + i, owners)
         pltpu.make_async_remote_copy(
             src_ref=message(other),
@@ -168,9 +176,8 @@
             device_id=(view, other),
             device_id_type=MESH,
         ).start()
-        return carried
-
-    lax.fori_loop(1, owners, send, 0)
+
+    for_others(owners, send)
 
 
 def send_views(views, block, landing, send_sem, recv_sem):
@@ -296,7 +303,7 @@
         64,
         forward,
         ((zero + 1.0,) * 4, (zero,) * 12, jnp.zeros((8, LANES), jnp.int32)),
-        unroll=16,
+        unroll=64,
     )
     residual = []
     for h in range(2):
@@ -326,7 +333,7 @@
                 weight[p, pl.ds(start, 8), :] = alpha * before
         return tuple(behind)
 
-    lax.fori_loop(0, 64, backward, (zero,) * 4, unroll=16)
+    lax.fori_loop(0, 64, backward, (zero,) * 4, unroll=64)
 
     pix = row_ids(LANES)
     col = lane_ids(LANES)
@@ -490,12 +497,14 @@
     by_slot,
     leaving_grads,
     arriving_grads,
+    arrived_views,
     grads,
     load_sems,
     store_sems,
     sems,
 ):
     view, me = lax.axis_index("view"), lax.axis_index("dev")
+    barrier, expected = greet(views, owners)
     copies = (
         (center_hbm, center_ref),
         (rows_hbm, rows_ref),
@@ -515,7 +524,6 @@
     ]
     for load in loads:
         load.start()
-    barrier, expected = greet(views, owners)
     lane = lane_ids()
     others = pl.ds(0, owners - 1)
     other_views = pl.ds(0, views - 1)
@@ -639,17 +647,6 @@
         return carried
 
     lax.fori_loop(0, 32, to_columns, 0, unroll=8)
-    wait_bytes(returned.at[others], sems.at[7])
-    values = [zero] * FEATS
-    for o in range(16):
-        block = returned[pl.ds(o, 8, stride=16), :]
-        chosen = lane // 8 == o
-        for f in range(FEATS):
-            values[f] = jnp.where(chosen, pick(block, 8 * f + lax.rem(lane, 8)), values[f])
-    for f in range(FEATS):
-        by_slot[view, 8 * f : 8 * f + 8, :] = values[f]
-    send_views(views, by_slot.at[view], lambda v: by_slot.at[v], sems.at[8], sems.at[9])
-
     for j in range(32):
         order_rows[j : j + 1, :] = order_lanes_ref[:, LANES * j : LANES * (j + 1)]
     wait_bytes(packed_landed.at[other_views], sems.at[3])
@@ -675,6 +672,35 @@
         for i in range(3)
     ]
 
+    wait_bytes(returned.at[others], sems.at[7])
+    values = [zero] * FEATS
+    for o in range(16):
+        block = returned[pl.ds(o, 8, stride=16), :]
+        chosen = lane // 8 == o
+        for f in range(FEATS):
+            values[f] = jnp.where(chosen, pick(block, 8 * f + lax.rem(lane, 8)), values[f])
+    for f in range(FEATS):
+        by_slot[view, 8 * f : 8 * f + 8, :] = values[f]
+    here = slot_high[3] // 8 == view
+    gone = [zero] * FEATS
+    for k in range(8):
+        chosen = slot_high[3] == 8 * view + k
+        for f in range(FEATS):
+            source = jnp.broadcast_to(by_slot[view, 8 * f + k : 8 * f + k + 1, :], (8, LANES))
+            gone[f] = jnp.where(chosen, pick(source, slot_low[3]), gone[f])
+    gone.append(jnp.where(here, (view + 1).astype(jnp.float32), zero))
+    rows = [found[7:8, :] for found in gone]
+    rows.append(jnp.zeros((LANES - len(rows), LANES), jnp.float32))
+    leaving_grads[...] = jnp.concatenate(rows, axis=0).T
+    send_each(
+        owners,
+        lambda d: leaving_grads.at[pl.ds(d, 1)],
+        lambda d: arriving_grads.at[pl.ds(d, 1)],
+        sems.at[10],
+        sems.at[11],
+    )
+    arriving_grads[pl.ds(me, 1), :] = leaving_grads[pl.ds(me, 1), :]
+    send_views(views, by_slot.at[view], lambda v: by_slot.at[v], sems.at[8], sems.at[9])
     wait_bytes(by_slot.at[other_views], sems.at[9])
 
     def collect(chunk):
@@ -693,7 +719,7 @@
 
     stores = []
 
-    def finish(chunk, feat_grads, view_of):
+    def finish(chunk, feat_grads, view_of, first, count):
         center = []
         for i in range(3):
             at = zero
@@ -704,7 +730,7 @@
         _, pull_back = jax.vjp(lambda *args: project(args, center), *arguments)
         for p, grad in enumerate(pull_back(list(feat_grads))):
             grads[pl.ds(chunk * 8 * PADDED + p, 8, stride=PADDED), :] = grad
-        for j in range(8 * chunk, 8 * chunk + 8):
+        for j in range(first, first + count):
             columns = slice(LANES * j, LANES * (j + 1))
             gradient = grads[PADDED * j : PADDED * j + PARAMS, :]
             new_one = BETA_ONE * new_first_ref[:, columns] + (1.0 - BETA_ONE) * gradient
@@ -714,7 +740,7 @@
             ) / (jnp.sqrt(new_two / bias_two) + ADAM_EPS)
             new_first_ref[:, columns] = new_one
             new_second_ref[:, columns] = new_two
-        columns = pl.ds(8 * LANES * chunk, 8 * LANES)
+        columns = pl.ds(LANES * first, LANES * count)
         for i, (source, place) in enumerate(
             (
                 (new_params_ref, new_params_hbm),
@@ -723,43 +749,40 @@
             )
         ):
             copy = pltpu.make_async_copy(
-                source.at[:, columns], place.at[:, columns], store_sems.at[3 * chunk + i]
+                source.at[:, columns], place.at[:, columns], store_sems.at[len(stores)]
             )
             copy.start()
             stores.append(copy)
 
+    for chunk in range(3):
+        finish(chunk, collect(chunk), slot_high[chunk] // 8, 8 * chunk, 8)
     last = collect(3)
     last_view = slot_high[3] // 8
-    rows = [found[7:8, :] for found in last] + [last_view[7:8, :].astype(jnp.float32)]
-    rows.append(jnp.zeros((LANES - len(rows), LANES), jnp.float32))
-    leaving_grads[...] = jnp.concatenate(rows, axis=0).T
-    send_each(
-        owners,
-        lambda d: leaving_grads.at[pl.ds(d, 1)],
-        lambda d: arriving_grads.at[pl.ds(d, 1)],
-        sems.at[10],
-        sems.at[11],
-    )
-    arriving_grads[pl.ds(me, 1), :] = leaving_grads[pl.ds(me, 1), :]
-    for chunk in range(3):
-        finish(chunk, collect(chunk), slot_high[chunk] // 8)
+    finish(3, last, last_view, 24, 7)
     wait_bytes(arriving_grads.at[others], sems.at[11])
-    arrived = arriving_grads[...].T
+    arrived_views[view] = arriving_grads[...].T[0:16, :]
+    send_views(
+        views, arrived_views.at[view], lambda v: arrived_views.at[v], sems.at[12], sems.at[13]
+    )
+    wait_bytes(arrived_views.at[other_views], sems.at[13])
+    arrived = arrived_views[0]
+    for v in range(1, views):
+        arrived = arrived + arrived_views[v]
     is_last = row_ids() == 7
     last = [
         jnp.where(is_last, jnp.broadcast_to(arrived[f : f + 1, :], (8, LANES)), last[f])
         for f in range(FEATS)
     ]
-    arrived_view = (arrived[FEATS : FEATS + 1, :] + 0.5).astype(jnp.int32)
-    finish(
-        3, last, jnp.where(is_last, jnp.broadcast_to(arrived_view, (8, LANES)), last_view)
-    )
+    arrived_view = (arrived[FEATS : FEATS + 1, :] + 0.5).astype(jnp.int32) - 1
+    last_view = jnp.where(is_last, jnp.broadcast_to(arrived_view, (8, LANES)), last_view)
+    finish(3, last, last_view, 31, 1)
     wait_bytes(landed.at[others], sems.at[0])
     wait_bytes(packed_landed.at[other_views], sems.at[2])
     wait_bytes(arriving.at[:, others], sems.at[4])
     wait_bytes(returned.at[others], sems.at[6])
     wait_bytes(by_slot.at[other_views], sems.at[8])
     wait_bytes(arriving_grads.at[others], sems.at[10])
+    wait_bytes(arrived_views.at[other_views], sems.at[12])
     for copy in stores:
         copy.wait()
 
@@ -860,10 +883,11 @@
             scratch(views, 8 * FEATS, LANES),
             scratch(owners, LANES),
             scratch(owners, LANES),
+            scratch(views, 16, LANES),
             scratch(32 * PADDED, LANES),
             pltpu.SemaphoreType.DMA((11,)),
-            pltpu.SemaphoreType.DMA((12,)),
-            pltpu.SemaphoreType.DMA((12,)),
+            pltpu.SemaphoreType.DMA((15,)),
+            pltpu.SemaphoreType.DMA((14,)),
         ],
         compiler_params=pltpu.CompilerParams(
             vmem_limit_bytes=VMEM_BYTES, collective_id=0, has_side_effects=True

time: 56.8 us -> 53.4 us (0.940)
  Pallas kernels: 56 us -> 52.4 us
    pallas_call x1, Pallas kernels: 53.2 us -> 49.6 us  [per_device(): pl.pallas_call(functools.partial(step_kernel, views, owners), out_shape=(...]
where the time goes in v5:
time: 53.4 us; the launch traced here: 53.2 us
  Pallas kernels  52.4 us (98%)
  between operations  0.8 us (1%)
    pallas_call x1, Pallas kernels, per_device(): pl.pallas_call(functools.partial(step_kernel, views, owners), out_shape=(...  49.6 us
    pallas_call x1, Pallas kernels, per_device(): pl.pallas_call(write_kernel, out_shape=(f32(PARAMS, 4096),) * 3, in_specs...  2.81 us

profile of v5, /device:TPU:1, one launch (start us, length us, event | category | flops | bytes accessed | tf_op | source)
XLA Modules:
  0.0 53.2 jit_solution(15121963281943339476)
XLA Ops:
  0.6 49.6 %step.1 = (f32[59,4096]{1,0:T(8,128)}, f32[59,4096]{1,0:T(8,128)}, f32[59,4096]{1,0:T(8,128)}) custom-call(f32[59,4096]{1,0:T(8,128)} %params_hbm.1, f32[59,4096]{1,0:T(8,128)} %first_hbm.1, f32[59,4096]{1,0:T(8,128)} %second_hbm.1, f32[1,3]{1,0:T(1,128)} %center_hbm.1, s32[1,1,1024]{2,1,0:T(1,128)} %rows_hbm.1, s32[1,4096]{1,0:T(1,128)} %order_hbm.1, ...), custom_call_target="tpu_custom_call" | custom-call | tf_op jit(solution)/shard_map/step/pallas_call | solution.py:841
  50.3 2.8 %write.1 = (f32[59,4096]{1,0:T(8,128)}, f32[59,4096]{1,0:T(8,128)}, f32[59,4096]{1,0:T(8,128)}) custom-call(f32[59,4096]{1,0:T(8,128)} %get-tuple-element.6.params, f32[59,4096]{1,0:T(8,128)} %get-tuple-element.7.first, f32[59,4096]{1,0:T(8,128)} %get-tuple-element.8.second), custom_call_target="tpu_custom_call" | custom-call | tf_op jit(solution)/shard_map/write/pallas_call | solution.py:908

commit v6 on v5

--- a/solution.py
+++ b/solution.py
@@ -242,6 +242,7 @@
     trans,
     gauss_grad,
     weight,
+    product,
     sums,
 ):
     lane = lane_ids()
@@ -329,8 +330,8 @@
                 gap = shade - behind[n]
                 behind[n] = behind[n] + alpha * gap
                 start = pl.multiple_of(512 * h + 8 * e, 8)
-                gauss_grad[p, pl.ds(start, 8), :] = before * gap * bell
-                weight[p, pl.ds(start, 8), :] = alpha * before
+                gauss_grad[pl.ds(start, 8), LANES * p : LANES * (p + 1)] = before * gap * bell
+                weight[pl.ds(start, 8), LANES * p : LANES * (p + 1)] = alpha * before
         return tuple(behind)
 
     lax.fori_loop(0, 64, backward, (zero,) * 4, unroll=64)
@@ -353,15 +354,15 @@
         stacked += [zero] * 9
         for_colors.append(jnp.concatenate(stacked, axis=0).T)
 
+    for_moments = jnp.concatenate(for_moments, axis=0)
+    for_colors = jnp.concatenate(for_colors, axis=0)
+    for part in range(4):
+        rows = slice(256 * part, 256 * (part + 1))
+        product[rows, :] = dot(gauss_grad[rows, :], for_moments) + dot(
+            weight[rows, :], for_colors
+        )
     for k in range(8):
-        rows = pl.ds(k, LANES, stride=8)
-        total = (
-            dot(gauss_grad[0, rows, :], for_moments[0])
-            + dot(gauss_grad[1, rows, :], for_moments[1])
-            + dot(weight[0, rows, :], for_colors[0])
-            + dot(weight[1, rows, :], for_colors[1])
-        )
-        sums[64 * k : 64 * k + 64, :] = total.T[0:64, :]
+        sums[64 * k : 64 * k + 64, :] = product[pl.ds(k, LANES, stride=8), :].T[0:64, :]
 
     s_0, s_u, s_v, s_uu, s_uv, s_vv = (sums[pl.ds(m, 8, stride=64), :] for m in range(6))
     d_colors = []
@@ -432,6 +433,16 @@
     return (place[0:32] + 0.5).astype(jnp.int32), (place[32:64] + 0.5).astype(jnp.int32)
 
 
+def adam(values, first, second, gradient):
+    bias_one = 1.0 - BETA_ONE**ADAM_STEP
+    bias_two = 1.0 - BETA_TWO**ADAM_STEP
+    sizes = step_sizes(row_ids(PADDED)[0:PARAMS])
+    new_one = BETA_ONE * first + (1.0 - BETA_ONE) * gradient
+    new_two = BETA_TWO * second + (1.0 - BETA_TWO) * gradient * gradient
+    updated = values - sizes * (new_one / bias_one) / (jnp.sqrt(new_two / bias_two) + ADAM_EPS)
+    return updated, new_one, new_two
+
+
 def per_tile(ref):
     values = ref[...]
     row, half_of = row_ids(), lane_ids() // 64
@@ -458,6 +469,7 @@
     new_params_hbm,
     new_first_hbm,
     new_second_hbm,
+    last_hbm,
     new_params_ref,
     new_first_ref,
     new_second_ref,
@@ -491,6 +503,7 @@
     trans,
     gauss_grad,
     weight,
+    product,
     sums,
     slot_grads,
     returned,
@@ -498,6 +511,7 @@
     leaving_grads,
     arriving_grads,
     arrived_views,
+    last,
     grads,
     load_sems,
     store_sems,
@@ -621,6 +635,7 @@
         trans,
         gauss_grad,
         weight,
+        product,
         sums,
     )
     send_each(
@@ -713,13 +728,10 @@
                 found[f] = jnp.where(chosen, pick(source, slot_low[chunk]), found[f])
         return found
 
-    bias_one = 1.0 - BETA_ONE**ADAM_STEP
-    bias_two = 1.0 - BETA_TWO**ADAM_STEP
-    sizes = step_sizes(row_ids(PADDED)[0:PARAMS])
-
     stores = []
 
-    def finish(chunk, feat_grads, view_of, first, count):
+    def finish(chunk, feat_grads, count):
+        view_of = slot_high[chunk] // 8
         center = []
         for i in range(3):
             at = zero
@@ -730,17 +742,20 @@
         _, pull_back = jax.vjp(lambda *args: project(args, center), *arguments)
         for p, grad in enumerate(pull_back(list(feat_grads))):
             grads[pl.ds(chunk * 8 * PADDED + p, 8, stride=PADDED), :] = grad
-        for j in range(first, first + count):
+        for j in range(8 * chunk, 8 * chunk + count):
             columns = slice(LANES * j, LANES * (j + 1))
             gradient = grads[PADDED * j : PADDED * j + PARAMS, :]
-            new_one = BETA_ONE * new_first_ref[:, columns] + (1.0 - BETA_ONE) * gradient
-            new_two = BETA_TWO * new_second_ref[:, columns] + (1.0 - BETA_TWO) * gradient * gradient
-            new_params_ref[:, columns] = new_params_ref[:, columns] - sizes * (
-                new_one / bias_one
-            ) / (jnp.sqrt(new_two / bias_two) + ADAM_EPS)
-            new_first_ref[:, columns] = new_one
-            new_second_ref[:, columns] = new_two
-        columns = pl.ds(LANES * first, LANES * count)
+            (
+                new_params_ref[:, columns],
+                new_first_ref[:, columns],
+                new_second_ref[:, columns],
+            ) = adam(
+                new_params_ref[:, columns],
+                new_first_ref[:, columns],
+                new_second_ref[:, columns],
+                gradient,
+            )
+        columns = pl.ds(8 * LANES * chunk, 8 * LANES)
         for i, (source, place) in enumerate(
             (
                 (new_params_ref, new_params_hbm),
@@ -754,11 +769,10 @@
             copy.start()
             stores.append(copy)
 
-    for chunk in range(3):
-        finish(chunk, collect(chunk), slot_high[chunk] // 8, 8 * chunk, 8)
-    last = collect(3)
-    last_view = slot_high[3] // 8
-    finish(3, last, last_view, 24, 7)
+    for chunk in range(4):
+        finish(chunk, collect(chunk), 8 if chunk < 3 else 7)
+    for v in range(views):
+        last[16 + 16 * v : 32 + 16 * v, :] = packed_landed[v]
     wait_bytes(arriving_grads.at[others], sems.at[11])
     arrived_views[view] = arriving_grads[...].T[0:16, :]
     send_views(
@@ -768,14 +782,10 @@
     arrived = arrived_views[0]
     for v in range(1, views):
         arrived = arrived + arrived_views[v]
-    is_last = row_ids() == 7
-    last = [
-        jnp.where(is_last, jnp.broadcast_to(arrived[f : f + 1, :], (8, LANES)), last[f])
-        for f in range(FEATS)
-    ]
-    arrived_view = (arrived[FEATS : FEATS + 1, :] + 0.5).astype(jnp.int32) - 1
-    last_view = jnp.where(is_last, jnp.broadcast_to(arrived_view, (8, LANES)), last_view)
-    finish(3, last, last_view, 31, 1)
+    last[0:16, :] = arrived
+    copy = pltpu.make_async_copy(last, last_hbm, store_sems.at[len(stores)])
+    copy.start()
+    stores.append(copy)
     wait_bytes(landed.at[others], sems.at[0])
     wait_bytes(packed_landed.at[other_views], sems.at[2])
     wait_bytes(arriving.at[:, others], sems.at[4])
@@ -788,21 +798,55 @@
 
 
 def write_kernel(
-    params, first, second, new_params, new_first, new_second, held, load_sems, store_sems
+    params,
+    first,
+    second,
+    last_hbm,
+    new_params,
+    new_first,
+    new_second,
+    held,
+    last,
+    grads,
+    load_sems,
+    store_sems,
 ):
-    loads, stores = [], []
-    for i, (source, place) in enumerate(
-        ((params, new_params), (first, new_first), (second, new_second))
-    ):
-        for part in range(4):
-            columns = pl.ds(1024 * part, 1024)
-            n = len(loads)
+    ends = ((params, new_params), (first, new_first), (second, new_second))
+    parts = [pl.ds(3968, 128)] + [pl.ds(1024 * k, 1024) for k in range(3)] + [pl.ds(3072, 896)]
+    loads, stores = [pltpu.make_async_copy(last_hbm, last, load_sems.at[0])], []
+    for columns in parts:
+        for i, (source, place) in enumerate(ends):
             middle = held.at[i, :, columns]
-            loads.append(pltpu.make_async_copy(source.at[:, columns], middle, load_sems.at[n]))
-            stores.append(pltpu.make_async_copy(middle, place.at[:, columns], store_sems.at[n]))
+            loads.append(
+                pltpu.make_async_copy(source.at[:, columns], middle, load_sems.at[len(loads)])
+            )
+            stores.append(
+                pltpu.make_async_copy(middle, place.at[:, columns], store_sems.at[len(stores)])
+            )
     for load in loads:
         load.start()
-    for load, store in zip(loads, stores):
+    for load in loads[0:4]:
+        load.wait()
+    columns = slice(3968, 4096)
+    view_of = (last[FEATS : FEATS + 1, :] + 0.5).astype(jnp.int32) - 1
+    center = []
+    for i in range(3):
+        at = jnp.zeros((1, LANES), jnp.float32)
+        for v in range(last.shape[0] // 16 - 1):
+            row = 16 * v + 24
+            one = jnp.broadcast_to(last[row : row + 1, i : i + 1], (1, LANES))
+            at = jnp.where(view_of == v, one, at)
+        center.append(at)
+    arguments = [held[0, p : p + 1, columns] for p in range(PARAMS)]
+    _, pull_back = jax.vjp(lambda *args: project(args, center), *arguments)
+    for p, grad in enumerate(pull_back([last[f : f + 1, :] for f in range(FEATS)])):
+        grads[p : p + 1, :] = grad
+    held[0, :, columns], held[1, :, columns], held[2, :, columns] = adam(
+        held[0, :, columns], held[1, :, columns], held[2, :, columns], grads[0:PARAMS, :]
+    )
+    for store in stores[0:3]:
+        store.start()
+    for load, store in zip(loads[4:], stores[3:]):
         load.wait()
         store.start()
     for store in stores:
@@ -840,9 +884,9 @@
     by_channel = target[0].transpose(1, 0, 2)
     updated = pl.pallas_call(
         functools.partial(step_kernel, views, owners),
-        out_shape=(f32(PARAMS, 4096),) * 3,
+        out_shape=(f32(PARAMS, 4096),) * 3 + (f32(16 + 16 * views, LANES),),
         in_specs=[HBM] * 10,
-        out_specs=(ANY,) * 3,
+        out_specs=(ANY,) * 4,
         scratch_shapes=[
             scratch(PARAMS, 4096),
             scratch(PARAMS, 4096),
@@ -875,8 +919,9 @@
             scratch(96, LANES),
             scratch(64, 4, 8, LANES),
             scratch(64, 4, 8, LANES),
-            scratch(2, 1024, LANES),
-            scratch(2, 1024, LANES),
+            scratch(1024, 2 * LANES),
+            scratch(1024, 2 * LANES),
+            scratch(1024, LANES),
             scratch(512, LANES),
             scratch(owners, LANES),
             scratch(owners, LANES),
@@ -884,9 +929,10 @@
             scratch(owners, LANES),
             scratch(owners, LANES),
             scratch(views, 16, LANES),
+            scratch(16 + 16 * views, LANES),
             scratch(32 * PADDED, LANES),
             pltpu.SemaphoreType.DMA((11,)),
-            pltpu.SemaphoreType.DMA((15,)),
+            pltpu.SemaphoreType.DMA((13,)),
             pltpu.SemaphoreType.DMA((14,)),
         ],
         compiler_params=pltpu.CompilerParams(
@@ -908,12 +954,14 @@
     return pl.pallas_call(
         write_kernel,
         out_shape=(f32(PARAMS, 4096),) * 3,
-        in_specs=[ANY] * 3,
+        in_specs=[ANY] * 4,
         out_specs=(HBM,) * 3,
         scratch_shapes=[
             scratch(3, PARAMS, 4096),
-            pltpu.SemaphoreType.DMA((12,)),
-            pltpu.SemaphoreType.DMA((12,)),
+            scratch(16 + 16 * views, LANES),
+            scratch(PADDED, LANES),
+            pltpu.SemaphoreType.DMA((16,)),
+            pltpu.SemaphoreType.DMA((15,)),
         ],
         compiler_params=pltpu.CompilerParams(vmem_limit_bytes=VMEM_BYTES),
         name="write",

time: 53.4 us -> 53.5 us (level)
  no operation moved by 1% of the time
where the time goes in v6:
time: 53.5 us; the launch traced here: 53.4 us
  Pallas kernels  52.6 us (98%)
  between operations  0.8 us (1%)
    pallas_call x1, Pallas kernels, per_device(): pl.pallas_call(functools.partial(step_kernel, views, owners), out_shape=(...  49.6 us
    pallas_call x1, Pallas kernels, per_device(): pl.pallas_call(write_kernel, out_shape=(f32(PARAMS, 4096),) * 3, in_specs...  2.94 us

profile of v6, /device:TPU:1, one launch (start us, length us, event | category | flops | bytes accessed | tf_op | source)
XLA Modules:
  0.0 53.4 jit_solution(6369794437732833727)
XLA Ops:
  0.6 49.6 %step.1 = (f32[59,4096]{1,0:T(8,128)}, f32[59,4096]{1,0:T(8,128)}, f32[59,4096]{1,0:T(8,128)}, f32[80,128]{1,0:T(8,128)}) custom-call(f32[59,4096]{1,0:T(8,128)} %params_hbm.1, f32[59,4096]{1,0:T(8,128)} %first_hbm.1, f32[59,4096]{1,0:T(8,128)} %second_hbm.1, f32[1,3]{1,0:T(1,128)} %center_hbm.1, s32[1,1,1024]{2,1,0:T(1,128)} %rows_hbm.1, ...), custom_call_target="tpu_custom_call" | custom-call | tf_op jit(solution)/shard_map/step/pallas_call | solution.py:885
  50.3 2.9 %write.1 = (f32[59,4096]{1,0:T(8,128)}, f32[59,4096]{1,0:T(8,128)}, f32[59,4096]{1,0:T(8,128)}) custom-call(f32[59,4096]{1,0:T(8,128)} %get-tuple-element.7.params, f32[59,4096]{1,0:T(8,128)} %get-tuple-element.8.first, f32[59,4096]{1,0:T(8,128)} %get-tuple-element.9.second, f32[80,128]{1,0:T(8,128)} %get-tuple-element.10.last_hbm), custom_call_target="tpu_custom_call" | custom-call | tf_op jit(solution)/shard_map/write/pallas_call | solution.py:954

commit v7 on v6

--- a/solution.py
+++ b/solution.py
@@ -512,6 +512,9 @@
     arriving_grads,
     arrived_views,
     last,
+    taken,
+    lanes_taken,
+    marked,
     grads,
     load_sems,
     store_sems,
@@ -687,7 +690,30 @@
         for i in range(3)
     ]
 
+    slots = (slot_high[3] * LANES + slot_low[3])[7:8, :].astype(jnp.float32)
+    slots = (jnp.broadcast_to(slots, (LANES, LANES)).T + 0.5).astype(jnp.int32)
+    column = lane_ids(LANES)
+    here = slots // 1024 == view
+    taken[...] = jnp.where((lax.rem(slots, 1024) // 8 == column) & here, 1.0, 0.0)
+    lanes_taken[...] = jnp.where(column < FEATS, column * 8 + lax.rem(slots, 8), 0)
+    marked[...] = jnp.where((column == FEATS) & here, (view + 1).astype(jnp.float32), 0.0)
+
     wait_bytes(returned.at[others], sems.at[7])
+    found = dot(taken[...], returned[...])
+    for i in range(16):
+        rows = slice(8 * i, 8 * i + 8)
+        leaving_grads[rows, :] = jnp.where(
+            lane < FEATS, pick(found[rows, :], lanes_taken[rows, :]), marked[rows, :]
+        )
+    send_each(
+        owners,
+        lambda d: leaving_grads.at[pl.ds(d, 1)],
+        lambda d: arriving_grads.at[pl.ds(d, 1)],
+        sems.at[10],
+        sems.at[11],
+    )
+    arriving_grads[pl.ds(me, 1), :] = leaving_grads[pl.ds(me, 1), :]
+
     values = [zero] * FEATS
     for o in range(16):
         block = returned[pl.ds(o, 8, stride=16), :]
@@ -696,25 +722,6 @@
             values[f] = jnp.where(chosen, pick(block, 8 * f + lax.rem(lane, 8)), values[f])
     for f in range(FEATS):
         by_slot[view, 8 * f : 8 * f + 8, :] = values[f]
-    here = slot_high[3] // 8 == view
-    gone = [zero] * FEATS
-    for k in range(8):
-        chosen = slot_high[3] == 8 * view + k
-        for f in range(FEATS):
-            source = jnp.broadcast_to(by_slot[view, 8 * f + k : 8 * f + k + 1, :], (8, LANES))
-            gone[f] = jnp.where(chosen, pick(source, slot_low[3]), gone[f])
-    gone.append(jnp.where(here, (view + 1).astype(jnp.float32), zero))
-    rows = [found[7:8, :] for found in gone]
-    rows.append(jnp.zeros((LANES - len(rows), LANES), jnp.float32))
-    leaving_grads[...] = jnp.concatenate(rows, axis=0).T
-    send_each(
-        owners,
-        lambda d: leaving_grads.at[pl.ds(d, 1)],
-        lambda d: arriving_grads.at[pl.ds(d, 1)],
-        sems.at[10],
-        sems.at[11],
-    )
-    arriving_grads[pl.ds(me, 1), :] = leaving_grads[pl.ds(me, 1), :]
     send_views(views, by_slot.at[view], lambda v: by_slot.at[v], sems.at[8], sems.at[9])
     wait_bytes(by_slot.at[other_views], sems.at[9])
 
@@ -769,8 +776,8 @@
             copy.start()
             stores.append(copy)
 
-    for chunk in range(4):
-        finish(chunk, collect(chunk), 8 if chunk < 3 else 7)
+    for chunk in range(2):
+        finish(chunk, collect(chunk), 8)
     for v in range(views):
         last[16 + 16 * v : 32 + 16 * v, :] = packed_landed[v]
     wait_bytes(arriving_grads.at[others], sems.at[11])
@@ -778,6 +785,8 @@
     send_views(
         views, arrived_views.at[view], lambda v: arrived_views.at[v], sems.at[12], sems.at[13]
     )
+    for chunk in (2, 3):
+        finish(chunk, collect(chunk), 8 if chunk < 3 else 7)
     wait_bytes(arrived_views.at[other_views], sems.at[13])
     arrived = arrived_views[0]
     for v in range(1, views):
@@ -930,6 +939,9 @@
             scratch(owners, LANES),
             scratch(views, 16, LANES),
             scratch(16 + 16 * views, LANES),
+            scratch(owners, LANES),
+            pltpu.VMEM((owners, LANES), jnp.int32),
+            scratch(owners, LANES),
             scratch(32 * PADDED, LANES),
             pltpu.SemaphoreType.DMA((11,)),
             pltpu.SemaphoreType.DMA((13,)),

time: 53.5 us -> 52.3 us (0.978)
  Pallas kernels: 52.6 us -> 51.4 us
    pallas_call x1, Pallas kernels: 49.6 us -> 48.4 us  [per_device(): pl.pallas_call(functools.partial(step_kernel, views, owners), out_shape=(...]
where the time goes in v7:
time: 52.3 us; the launch traced here: 52.2 us
  Pallas kernels  51.4 us (98%)
  between operations  0.8 us (2%)
    pallas_call x1, Pallas kernels, per_device(): pl.pallas_call(functools.partial(step_kernel, views, owners), out_shape=(...  48.4 us
    pallas_call x1, Pallas kernels, per_device(): pl.pallas_call(write_kernel, out_shape=(f32(PARAMS, 4096),) * 3, in_specs...  2.94 us

profile of v7, /device:TPU:1, one launch (start us, length us, event | category | flops | bytes accessed | tf_op | source)
XLA Modules:
  0.0 52.2 jit_solution(9619979379953556199)
XLA Ops:
  0.6 48.4 %step.1 = (f32[59,4096]{1,0:T(8,128)}, f32[59,4096]{1,0:T(8,128)}, f32[59,4096]{1,0:T(8,128)}, f32[80,128]{1,0:T(8,128)}) custom-call(f32[59,4096]{1,0:T(8,128)} %params_hbm.1, f32[59,4096]{1,0:T(8,128)} %first_hbm.1, f32[59,4096]{1,0:T(8,128)} %second_hbm.1, f32[1,3]{1,0:T(1,128)} %center_hbm.1, s32[1,1,1024]{2,1,0:T(1,128)} %rows_hbm.1, ...), custom_call_target="tpu_custom_call" | custom-call | tf_op jit(solution)/shard_map/step/pallas_call | solution.py:894
  49.1 2.9 %write.1 = (f32[59,4096]{1,0:T(8,128)}, f32[59,4096]{1,0:T(8,128)}, f32[59,4096]{1,0:T(8,128)}) custom-call(f32[59,4096]{1,0:T(8,128)} %get-tuple-element.7.params, f32[59,4096]{1,0:T(8,128)} %get-tuple-element.8.first, f32[59,4096]{1,0:T(8,128)} %get-tuple-element.9.second, f32[80,128]{1,0:T(8,128)} %get-tuple-element.10.last_hbm), custom_call_target="tpu_custom_call" | custom-call | tf_op jit(solution)/shard_map/write/pallas_call | solution.py:966

commit v8 on v7

--- a/solution.py
+++ b/solution.py
@@ -521,7 +521,6 @@
     sems,
 ):
     view, me = lax.axis_index("view"), lax.axis_index("dev")
-    barrier, expected = greet(views, owners)
     copies = (
         (center_hbm, center_ref),
         (rows_hbm, rows_ref),
@@ -539,7 +538,10 @@
         pltpu.make_async_copy(source, place, load_sems.at[i])
         for i, (source, place) in enumerate(copies)
     ]
-    for load in loads:
+    for load in loads[0:3]:
+        load.start()
+    barrier, expected = greet(views, owners)
+    for load in loads[3:]:
         load.start()
     lane = lane_ids()
     others = pl.ds(0, owners - 1)
@@ -626,12 +628,13 @@
     odd = list_rows[pl.ds(1, 8, stride=2), :]
     lists = jnp.where(lane < 64, even, pick(odd, lax.rem(lane, 64)))
 
+    counts, ids = per_tile(counts_ref), per_tile(ids_ref)
     wait_bytes(landed.at[others], sems.at[1])
     render(
         landed,
         lists,
-        per_tile(counts_ref),
-        per_tile(ids_ref),
+        counts,
+        ids,
         wanted,
         slot_grads,
         gauss,

time: 52.3 us -> 51.8 us (level)
  Pallas kernels: 51.4 us -> 50.8 us
    pallas_call x1, Pallas kernels: 48.4 us -> 47.9 us  [per_device(): pl.pallas_call(functools.partial(step_kernel, views, owners), out_shape=(...]
where the time goes in v8:
time: 51.8 us; the launch traced here: 51.6 us
  Pallas kernels  50.8 us (98%)
  between operations  0.8 us (2%)
    pallas_call x1, Pallas kernels, per_device(): pl.pallas_call(functools.partial(step_kernel, views, owners), out_shape=(...  47.9 us
    pallas_call x1, Pallas kernels, per_device(): pl.pallas_call(write_kernel, out_shape=(f32(PARAMS, 4096),) * 3, in_specs...  2.94 us

profile of v8, /device:TPU:1, one launch (start us, length us, event | category | flops | bytes accessed | tf_op | source)
XLA Modules:
  0.0 51.6 jit_solution(1737241428358064260)
XLA Ops:
  0.6 47.9 %step.1 = (f32[59,4096]{1,0:T(8,128)}, f32[59,4096]{1,0:T(8,128)}, f32[59,4096]{1,0:T(8,128)}, f32[80,128]{1,0:T(8,128)}) custom-call(f32[59,4096]{1,0:T(8,128)} %params_hbm.1, f32[59,4096]{1,0:T(8,128)} %first_hbm.1, f32[59,4096]{1,0:T(8,128)} %second_hbm.1, f32[1,3]{1,0:T(1,128)} %center_hbm.1, s32[1,1,1024]{2,1,0:T(1,128)} %rows_hbm.1, ...), custom_call_target="tpu_custom_call" | custom-call | tf_op jit(solution)/shard_map/step/pallas_call | solution.py:897
  48.5 2.9 %write.1 = (f32[59,4096]{1,0:T(8,128)}, f32[59,4096]{1,0:T(8,128)}, f32[59,4096]{1,0:T(8,128)}) custom-call(f32[59,4096]{1,0:T(8,128)} %get-tuple-element.7.params, f32[59,4096]{1,0:T(8,128)} %get-tuple-element.8.first, f32[59,4096]{1,0:T(8,128)} %get-tuple-element.9.second, f32[80,128]{1,0:T(8,128)} %get-tuple-element.10.last_hbm), custom_call_target="tpu_custom_call" | custom-call | tf_op jit(solution)/shard_map/write/pallas_call | solution.py:969
